TPU v7x, 32 devices: a whole 2x2x4 slice. The times are simulated.
32 devices in a mesh: row: 4 (over z), col: 8 (over y, x, core).
Axes of the slice: x: 2, y: 2, z: 4, core: 2. Of those that a mesh axis runs over, the one named last changes fastest.
Arguments:
- gate_pre: bfloat16 [1024, 16384], P('row', 'col'), may hold values from -8 to 8
- up_pre: bfloat16 [1024, 16384], P('row', 'col'), may hold values from -6 to 6
- down_t: bfloat16 [4096, 16384], P('row', 'col'), may hold values from -0.09375 to 0.09375
- grad_out: bfloat16 [1024, 4096], P('row', 'col'), may hold values from -6 to 6
Outputs:
- gate_grad: bfloat16 [1024, 16384], P('row', 'col')
- up_grad: bfloat16 [1024, 16384], P('row', 'col')
- weight_grad: bfloat16 [4096, 16384], P('row', 'col')
All inputs are finite; a program needn't handle non-finite values.
Results may differ from a plain program's by a relative error of at most 0.0049.
Values may be sent and summed in bfloat16 or wider, within the bound.
No kernel may reach another device: no remote copies, remote signals or barrier semaphores. Data moves between devices by JAX's collectives and lax.ppermute only.
A program may use at most 128 MiB of HBM per device.

v0:
```python
import jax
import jax.numpy as jnp
from jax import lax
from jax.experimental import pallas as pl
from jax.experimental.pallas import tpu as pltpu
from jax.sharding import PartitionSpec as P

PARTS = 2


def after(value, first):
    return lax.optimization_barrier((value, first))[0]


def lay_strips(near, far):
    chips = len(near)
    rows, strip, width = near[0].shape

    def kernel(*refs):
        row, col = lax.axis_index("row"), lax.axis_index("col")
        out_ref = refs[-1]
        for at, ref in enumerate(refs[:-1]):
            core, chip = at // chips, at % chips
            lane = pl.multiple_of(((col & 1) ^ core) * width, width)
            for group in range(rows):
                slot = lax.rem((row ^ group) + rows - row, rows)
                start = (slot * chips + (col // 2 ^ chip)) * strip
                out_ref[pl.ds(pl.multiple_of(start, strip), strip), pl.ds(lane, width)] = ref[group]

    return pl.pallas_call(
        kernel,
        out_shape=jax.ShapeDtypeStruct((rows * chips * strip, 2 * width), near[0].dtype),
        in_specs=[pl.BlockSpec(memory_space=pltpu.VMEM)] * 2 * chips,
        out_specs=pl.BlockSpec(memory_space=pltpu.VMEM),
        compiler_params=pltpu.CompilerParams(vmem_limit_bytes=32 * 2**20),
        name="lay_strips",
    )(*near, *far)


def add_share(sources, cot, down_t, start, mine):
    span = sum(count for _, _, count in sources)
    like = sources[0][0]
    width = like.shape[1]
    tile = 512 if width % 512 == 0 else width

    def kernel(*refs):
        got_refs, (cot_ref, down_ref, out_ref) = refs[: len(sources)], refs[len(sources) :]
        is_sum = mine(lax.axis_index("row"))
        places, at = [], 0
        for ref, (_, first, count) in zip(got_refs, sources):
            places.append((ref, slice(first, first + count), slice(at, at + count)))
            at += count

        @pl.when(is_sum)
        def _():
            tokens = cot_ref[start : start + span, :]
            for at in range(0, width, tile):
                cut = slice(at, at + tile)
                share = jnp.dot(tokens, down_ref[:, cut], preferred_element_type=jnp.float32)
                for ref, source, here in places:
                    total = ref[source, cut].astype(jnp.float32) + share[here]
                    out_ref[here, cut] = total.astype(out_ref.dtype)

        @pl.when(jnp.logical_not(is_sum))
        def _():
            for ref, source, here in places:
                out_ref[here, :] = ref[source, :]

    whole = pl.BlockSpec(memory_space=pltpu.VMEM)
    return pl.pallas_call(
        kernel,
        out_shape=jax.ShapeDtypeStruct((span, width), like.dtype),
        in_specs=[whole] * (2 + len(sources)),
        out_specs=whole,
        compiler_params=pltpu.CompilerParams(vmem_limit_bytes=32 * 2**20),
        cost_estimate=pl.CostEstimate(
            flops=2 * span * down_t.size, bytes_accessed=4 * span * width, transcendentals=0
        ),
        name="add_share",
    )(*(array for array, _, _ in sources), cot, down_t)


def rows_of(pieces, start, count):
    found, at = [], 0
    for piece in pieces:
        low, high = max(start, at), min(start + count, at + piece.shape[0])
        if low < high:
            found.append((piece, low - at, high - low))
        at += piece.shape[0]
    return found


def weight_product(cot, own, fore, back, scale):
    rows = len(fore) + 1
    tok_rows, width = own.shape
    tile = 512 if width % 512 == 0 else width
    flat = [piece for pieces in fore + back for piece in pieces]

    def kernel(cot_ref, own_ref, *refs):
        ends, (out_ref, hidden_ref) = iter(refs[: len(flat)]), refs[len(flat) :]
        fore_refs, back_refs = ([[next(ends) for _ in pieces] for pieces in way] for way in (fore, back))
        row = lax.axis_index("row")

        def place(pieces, start, cut):
            for piece in pieces:
                hidden_ref[start : start + piece.shape[0], :] = piece[:, cut].astype(hidden_ref.dtype)
                start += piece.shape[0]

        @pl.loop(0, width // tile)
        def _(at):
            cut = pl.ds(pl.multiple_of(at * tile, tile), tile)
            place([own_ref], 0, cut)
            for slot in range(1, rows):
                for here, pieces in (
                    (row + slot < rows, back_refs[slot - 1]),
                    (row + slot >= rows, fore_refs[rows - slot - 1]),
                ):
                    pl.when(here)(lambda pieces=pieces, slot=slot: place(pieces, slot * tok_rows, cut))
            total = lax.dot_general(
                cot_ref[...],
                hidden_ref[...],
                (((0,), (0,)), ((), ())),
                preferred_element_type=jnp.float32,
            )
            out_ref[:, cut] = (total * scale).astype(out_ref.dtype)

    whole = pl.BlockSpec(memory_space=pltpu.VMEM)
    return pl.pallas_call(
        kernel,
        out_shape=jax.ShapeDtypeStruct((cot.shape[1], width), jnp.bfloat16),
        in_specs=[whole] * (2 + len(flat)),
        out_specs=whole,
        scratch_shapes=[pltpu.VMEM((cot.shape[0], tile), jnp.bfloat16)],
        compiler_params=pltpu.CompilerParams(vmem_limit_bytes=32 * 2**20),
        cost_estimate=pl.CostEstimate(
            flops=2 * cot.size * width, bytes_accessed=4 * cot.shape[0] * width, transcendentals=0
        ),
        name="weight_product",
    )(cot, own, *flat)


def finish(gate_pre, up_pre, share, fore, back, start, grads):
    span, width = fore.shape
    tile = 512 if width % 512 == 0 else width
    old = () if grads is None else tuple(grads)

    def kernel(*refs):
        gate_ref, up_ref, share_ref, fore_ref, back_ref = refs[:5]
        outs, parts, sems = refs[5 + len(old) : 7 + len(old)], refs[-3:-1], refs[-1]
        here = slice(start, start + span)
        copies = []
        for at in range(0, width, tile):
            cut = slice(at, at + tile)
            grad = share_ref[here, cut] + fore_ref[:, cut].astype(jnp.float32) + back_ref[:, cut].astype(jnp.float32)
            gate = gate_ref[here, cut].astype(jnp.float32)
            sigmoid = jax.nn.sigmoid(gate)
            slope = sigmoid * (1.0 + gate * (1.0 - sigmoid))
            parts[0][:, cut] = (grad * up_ref[here, cut].astype(jnp.float32) * slope).astype(jnp.bfloat16)
            parts[1][:, cut] = (grad * (gate * sigmoid)).astype(jnp.bfloat16)
            for which, (part, out) in enumerate(zip(parts, outs)):
                copy = pltpu.make_async_copy(part.at[:, cut], out.at[here, cut], sems.at[which, at // tile])
                copy.start()
                copies.append(copy)
        for copy in copies:
            copy.wait()

    whole, anywhere = pl.BlockSpec(memory_space=pltpu.VMEM), pl.BlockSpec(memory_space=pl.ANY)
    return pl.pallas_call(
        kernel,
        out_shape=[jax.ShapeDtypeStruct(gate_pre.shape, jnp.bfloat16)] * 2,
        in_specs=[whole] * 5 + [anywhere] * len(old),
        out_specs=[anywhere] * 2,
        scratch_shapes=[pltpu.VMEM((span, width), jnp.bfloat16)] * 2
        + [pltpu.SemaphoreType.DMA((2, width // tile))],
        input_output_aliases={5 + at: at for at in range(len(old))},
        compiler_params=pltpu.CompilerParams(vmem_limit_bytes=32 * 2**20),
        cost_estimate=pl.CostEstimate(flops=20 * span * width, bytes_accessed=8 * span * width, transcendentals=span * width),
        name="finish",
    )(gate_pre, up_pre, share, fore, back, *old)


def swap(value, bits):
    return lax.ppermute(value, "col", [(at, at ^ bits) for at in range(lax.axis_size("col"))])


def spread_cotangent(grad_out, hidden, first):
    rows, cols = lax.axis_size("row"), lax.axis_size("col")
    row = lax.axis_index("row")
    tok_rows, width = grad_out.shape
    per_row = cols // rows
    if (rows, cols) != (4, 8):
        pairs = [
            (src * cols + per_row * dst + part, dst * cols + per_row * ((src - dst) % rows) + part)
            for src in range(rows)
            for dst in range(rows)
            for part in range(per_row)
        ]
        moved = lax.ppermute(grad_out, ("row", "col"), pairs)
        blocks = lax.all_gather(moved, "col", axis=0)
        blocks = blocks.reshape(rows, per_row, tok_rows, width)
        return blocks.transpose(0, 2, 1, 3).reshape(rows * tok_rows, per_row * width)
    strip = tok_rows * 2 // cols
    chip = lax.axis_index("col") // 2

    def quarter(bits):
        piece = lax.dynamic_slice_in_dim(grad_out, (chip ^ bits) * strip, strip, 0)
        return swap(piece, 2 * bits) if bits else piece

    wide = after([quarter(bits) for bits in range(cols // 2)], hidden[0])

    def across(bits):
        piece = lax.dynamic_index_in_dim(jnp.stack(wide), chip ^ row ^ bits, 0, keepdims=False)
        return lax.ppermute(piece, "row", [(at, at ^ bits) for at in range(rows)]) if bits else piece

    tall = [across(bits) for bits in range(rows - 1, -1, -1)]
    tall = jnp.stack(tall[::-1])
    near = [tall, swap(tall, 2), swap(tall, 4), swap(tall, 6)]
    near[-1] = after(near[-1], first)
    return lay_strips(near, [swap(block, 1) for block in near])


def per_device(gate_pre, up_pre, down_t, grad_out):
    rows = lax.axis_size("row")
    row = lax.axis_index("row")
    tok_rows, width = gate_pre.shape
    norm_scale = (tok_rows * rows) ** (-0.5)
    wire = jnp.bfloat16 if rows <= 4 else jnp.float32
    ahead = [(at, at + 1) for at in range(rows - 1)]
    behind = [(at + 1, at) for at in range(rows - 1)]
    span = tok_rows // PARTS

    hidden, fore, back = [], [None, []], [None, []]
    for start, count in ((0, span), (span, span)):
        gate_cut = gate_pre[start : start + count].astype(jnp.float32)
        up_cut = up_pre[start : start + count].astype(jnp.float32)
        hidden.append((gate_cut * jax.nn.sigmoid(gate_cut) * up_cut).astype(jnp.bfloat16))
        fore[1].append(lax.ppermute(hidden[-1].astype(wire), "row", ahead))
        back[1].append(lax.ppermute(hidden[-1].astype(wire), "row", behind))

    cot = spread_cotangent(grad_out, hidden, (fore[1][:1], back[1][:1]))
    turn = hidden[0]
    for step in range(2, rows + 1):
        fore.append([None] * PARTS)
        back.append([None] * PARTS)
        for at in range(PARTS):
            for ends, slot, mine, pairs in (
                (fore, rows + 1 - step, lambda row, step=step: step > row + 1, ahead),
                (back, step - 1, lambda row, step=step: step > rows - row, behind),
            ):
                sources = [
                    (after(piece, turn), first, count)
                    for piece, first, count in rows_of(ends[step - 1], at * span, span)
                ]
                turn = add_share(sources, cot, down_t, slot * tok_rows + at * span, mine)
                ends[step][at] = lax.ppermute(turn, "row", pairs)
        late = turn

    weight_grad = weight_product(cot, jnp.concatenate(hidden), fore[1:rows], back[1:rows], norm_scale)

    own_share = jnp.dot(after(cot[:tok_rows], late), down_t, preferred_element_type=jnp.float32)
    own_share, gate_again, up_again = after((own_share, gate_pre, up_pre), turn)
    grads = None
    for at in range(PARTS):
        grads = finish(gate_again, up_again, own_share, fore[rows][at], back[rows][at], at * span, grads)
    return *grads, weight_grad


def solution(mesh):
    specs = (P("row", "col"),) * 4
    return jax.shard_map(
        per_device, mesh=mesh, in_specs=specs, out_specs=specs[:3], check_vma=False
    )
```

profile of v0, /device:TPU:0, one launch (start us, length us, event | category | flops | bytes accessed | tf_op | source)
XLA Modules:
  0.0 118.4 jit_solution(3044472641880846325)
XLA Ops:
  1.6 3.0 %collective-permute-start = (bf16[64,512]{1,0:T(8,128)(2,1)S(1)}, bf16[64,512]{1,0:T(8,128)(2,1)S(1)}, u32[]{:S(2)}, u32[]{:S(2)}) collective-permute-start(bf16[64,512]{1,0:T(8,128)(2,1)S(1)} %get-tuple-element.60), channel_id=1, source_target_pairs={{0,2},{1,3},{2,0},{3,1},{4,6},{5,7},{6,4},{7,5},{8,10},{9,11},{10,... | collective-permute-start | bytes 196616 | tf_op jit(solution)/shard_map/ppermute | solution.py:183
  4.6 1.5 %collective-permute-start.1 = (bf16[64,512]{1,0:T(8,128)(2,1)S(1)}, bf16[64,512]{1,0:T(8,128)(2,1)S(1)}, u32[]{:S(2)}, u32[]{:S(2)}) collective-permute-start(bf16[64,512]{1,0:T(8,128)(2,1)S(1)} %get-tuple-element.62), channel_id=1, source_target_pairs={{0,4},{1,5},{2,6},{3,7},{4,0},{5,1},{6,2},{7,3},{8,12},{9,13},{10,... | collective-permute-start | bytes 196616 | tf_op jit(solution)/shard_map/ppermute | solution.py:183
  6.2 2.2 %fusion.8 = (bf16[128,2048]{1,0:T(8,128)(2,1)S(1)}, bf16[128,2048]{1,0:T(8,128)(2,1)S(1)}) fusion(bf16[256,2048]{1,0:T(8,128)(2,1)} %refs_1_.1, bf16[256,2048]{1,0:T(8,128)(2,1)} %refs_0_.1), kind=kLoop, calls=%fused_computation.13 | loop fusion | flops 4194304 | bytes 3145728 | tf_op jit(solution)/shard_map/convert_element_type | solution.py:236
  8.9 2.4 %collective-permute-done.2 = bf16[64,512]{1,0:T(8,128)(2,1)S(1)} collective-permute-done((bf16[64,512]{1,0:T(8,128)(2,1)S(1)}, bf16[64,512]{1,0:T(8,128)(2,1)S(1)}, u32[]{:S(2)}, u32[]{:S(2)}) %collective-permute-start.2) | collective-permute-done | bytes 65568 | tf_op jit(solution)/shard_map/ppermute | solution.py:183
  11.4 1.6 %collective-permute-start.3 = (bf16[64,512]{1,0:T(8,128)(2,1)S(1)}, bf16[64,512]{1,0:T(8,128)(2,1)S(1)}, u32[]{:S(2)}, u32[]{:S(2)}) collective-permute-start(bf16[64,512]{1,0:T(8,128)(2,1)S(1)} %get-tuple-element.58), channel_id=1, source_target_pairs={{0,8},{8,0},{16,24},{24,16},{1,9},{9,1},{17,25},{25,17},{2,10},{10... | collective-permute-start | bytes 196616 | tf_op jit(solution)/shard_map/ppermute | solution.py:213
  13.0 2.6 %collective-permute-start.4 = (bf16[64,512]{1,0:T(8,128)(2,1)S(1)}, bf16[64,512]{1,0:T(8,128)(2,1)S(1)}, u32[]{:S(2)}, u32[]{:S(2)}) collective-permute-start(bf16[64,512]{1,0:T(8,128)(2,1)S(1)} %get-tuple-element.57), channel_id=1, source_target_pairs={{0,16},{8,24},{16,0},{24,8},{1,17},{9,25},{17,1},{25,9},{2,18},{10... | collective-permute-start | bytes 196616 | tf_op jit(solution)/shard_map/ppermute | solution.py:213
  17.1 4.6 %collective-permute-start.9 = (bf16[128,2048]{1,0:T(8,128)(2,1)S(1)}, bf16[128,2048]{1,0:T(8,128)(2,1)S(1)}, u32[]{:S(2)}, u32[]{:S(2)}) collective-permute-start(bf16[128,2048]{1,0:T(8,128)(2,1)S(1)} %get-tuple-element.54), channel_id=1, source_target_pairs={{0,8},{8,16},{16,24},{1,9},{9,17},{17,25},{2,10},{10,18},{18,26},{... | collective-permute-start | bytes 1572872 | tf_op jit(solution)/shard_map/ppermute | solution.py:237
  23.1 1.5 %collective-permute-start.6 = (bf16[4,64,512]{2,1,0:T(8,128)(2,1)S(1)}, bf16[4,64,512]{2,1,0:T(8,128)(2,1)S(1)}, u32[]{:S(2)}, u32[]{:S(2)}) collective-permute-start(bf16[4,64,512]{2,1,0:T(8,128)(2,1)S(1)} %pad_maximum_fusion.2.refs_0_), channel_id=1, source_target_pairs={{0,2},{1,3},{2,0},{3,1},{4,6},{5,7},{6,4},{7,5},{8,10},{9,11},{10,... | collective-permute-start | bytes 786440 | tf_op jit(solution)/shard_map/ppermute | solution.py:183
  24.5 1.5 %collective-permute-start.7 = (bf16[4,64,512]{2,1,0:T(8,128)(2,1)S(1)}, bf16[4,64,512]{2,1,0:T(8,128)(2,1)S(1)}, u32[]{:S(2)}, u32[]{:S(2)}) collective-permute-start(bf16[4,64,512]{2,1,0:T(8,128)(2,1)S(1)} %pad_maximum_fusion.2.refs_0_), channel_id=1, source_target_pairs={{0,4},{1,5},{2,6},{3,7},{4,0},{5,1},{6,2},{7,3},{8,12},{9,13},{10,... | collective-permute-start | bytes 786440 | tf_op jit(solution)/shard_map/ppermute | solution.py:183
  26.1 4.9 %collective-permute-done.8.refs_3_ = bf16[4,64,512]{2,1,0:T(8,128)(2,1)S(1)} collective-permute-done((bf16[4,64,512]{2,1,0:T(8,128)(2,1)S(1)}, bf16[4,64,512]{2,1,0:T(8,128)(2,1)S(1)}, u32[]{:S(2)}, u32[]{:S(2)}) %collective-permute-start.8) | collective-permute-done | bytes 262176 | tf_op jit(solution)/shard_map/ppermute | solution.py:183
  30.9 1.8 %collective-permute-done.6.refs_1_ = bf16[4,64,512]{2,1,0:T(8,128)(2,1)S(1)} collective-permute-done((bf16[4,64,512]{2,1,0:T(8,128)(2,1)S(1)}, bf16[4,64,512]{2,1,0:T(8,128)(2,1)S(1)}, u32[]{:S(2)}, u32[]{:S(2)}) %collective-permute-start.6) | collective-permute-done | bytes 262176 | tf_op jit(solution)/shard_map/ppermute | solution.py:183
  32.7 2.6 %collective-permute-start.16 = (bf16[128,2048]{1,0:T(8,128)(2,1)S(1)}, bf16[128,2048]{1,0:T(8,128)(2,1)S(1)}, u32[]{:S(2)}, u32[]{:S(2)}) collective-permute-start(bf16[128,2048]{1,0:T(8,128)(2,1)S(1)} %get-tuple-element.53), channel_id=1, source_target_pairs={{0,8},{8,16},{16,24},{1,9},{9,17},{17,25},{2,10},{10,18},{18,26},{... | collective-permute-start | bytes 1572872 | tf_op jit(solution)/shard_map/ppermute | solution.py:237
  39.9 3.9 %collective-permute-start.20 = (bf16[128,2048]{1,0:T(8,128)(2,1)S(1)}, bf16[128,2048]{1,0:T(8,128)(2,1)S(1)}, u32[]{:S(2)}, u32[]{:S(2)}) collective-permute-start(bf16[128,2048]{1,0:T(8,128)(2,1)S(1)} %add_share.12), channel_id=1, source_target_pairs={{0,8},{8,16},{16,24},{1,9},{9,17},{17,25},{2,10},{10,18},{18,26},{... | collective-permute-start | bytes 1572872 | tf_op jit(solution)/shard_map/ppermute | solution.py:255
  47.3 3.7 %collective-permute-start.18 = (bf16[128,2048]{1,0:T(8,128)(2,1)S(1)}, bf16[128,2048]{1,0:T(8,128)(2,1)S(1)}, u32[]{:S(2)}, u32[]{:S(2)}) collective-permute-start(bf16[128,2048]{1,0:T(8,128)(2,1)S(1)} %add_share.14), channel_id=1, source_target_pairs={{0,8},{8,16},{16,24},{1,9},{9,17},{17,25},{2,10},{10,18},{18,26},{... | collective-permute-start | bytes 1572872 | tf_op jit(solution)/shard_map/ppermute | solution.py:255
  52.4 5.4 %collective-permute-done.20.refs_0_.refs_2_ = bf16[128,2048]{1,0:T(8,128)(2,1)S(1)} collective-permute-done((bf16[128,2048]{1,0:T(8,128)(2,1)S(1)}, bf16[128,2048]{1,0:T(8,128)(2,1)S(1)}, u32[]{:S(2)}, u32[]{:S(2)}) %collective-permute-start.20) | collective-permute-done | bytes 524320 | tf_op jit(solution)/shard_map/ppermute | solution.py:255
  58.5 4.4 %collective-permute-start.24 = (bf16[128,2048]{1,0:T(8,128)(2,1)S(1)}, bf16[128,2048]{1,0:T(8,128)(2,1)S(1)}, u32[]{:S(2)}, u32[]{:S(2)}) collective-permute-start(bf16[128,2048]{1,0:T(8,128)(2,1)S(1)} %add_share.16), channel_id=1, source_target_pairs={{0,8},{8,16},{16,24},{1,9},{9,17},{17,25},{2,10},{10,18},{18,26},{... | collective-permute-start | bytes 1572872 | tf_op jit(solution)/shard_map/ppermute | solution.py:255
  64.3 4.7 %collective-permute-done.18.refs_0_.refs_3_ = bf16[128,2048]{1,0:T(8,128)(2,1)S(1)} collective-permute-done((bf16[128,2048]{1,0:T(8,128)(2,1)S(1)}, bf16[128,2048]{1,0:T(8,128)(2,1)S(1)}, u32[]{:S(2)}, u32[]{:S(2)}) %collective-permute-start.18) | collective-permute-done | bytes 524320 | tf_op jit(solution)/shard_map/ppermute | solution.py:255
  69.8 4.4 %collective-permute-start.22 = (bf16[128,2048]{1,0:T(8,128)(2,1)S(1)}, bf16[128,2048]{1,0:T(8,128)(2,1)S(1)}, u32[]{:S(2)}, u32[]{:S(2)}) collective-permute-start(bf16[128,2048]{1,0:T(8,128)(2,1)S(1)} %add_share.18), channel_id=1, source_target_pairs={{0,8},{8,16},{16,24},{1,9},{9,17},{17,25},{2,10},{10,18},{18,26},{... | collective-permute-start | bytes 1572872 | tf_op jit(solution)/shard_map/ppermute | solution.py:255
  75.7 4.6 %collective-permute-done.24.refs_0_.refs_4_ = bf16[128,2048]{1,0:T(8,128)(2,1)S(1)} collective-permute-done((bf16[128,2048]{1,0:T(8,128)(2,1)S(1)}, bf16[128,2048]{1,0:T(8,128)(2,1)S(1)}, u32[]{:S(2)}, u32[]{:S(2)}) %collective-permute-start.24) | collective-permute-done | bytes 524320 | tf_op jit(solution)/shard_map/ppermute | solution.py:255
  81.0 4.4 %collective-permute-start.27 = (bf16[128,2048]{1,0:T(8,128)(2,1)S(1)}, bf16[128,2048]{1,0:T(8,128)(2,1)S(1)}, u32[]{:S(2)}, u32[]{:S(2)}) collective-permute-start(bf16[128,2048]{1,0:T(8,128)(2,1)S(1)} %add_share.20), channel_id=1, source_target_pairs={{0,8},{8,16},{16,24},{1,9},{9,17},{17,25},{2,10},{10,18},{18,26},{... | collective-permute-start | bytes 1572872 | tf_op jit(solution)/shard_map/ppermute | solution.py:255
  86.8 4.7 %collective-permute-done.22.refs_0_.refs_5_ = bf16[128,2048]{1,0:T(8,128)(2,1)S(1)} collective-permute-done((bf16[128,2048]{1,0:T(8,128)(2,1)S(1)}, bf16[128,2048]{1,0:T(8,128)(2,1)S(1)}, u32[]{:S(2)}, u32[]{:S(2)}) %collective-permute-start.22) | collective-permute-done | bytes 524320 | tf_op jit(solution)/shard_map/ppermute | solution.py:255
  92.2 4.4 %collective-permute-start.25 = (bf16[128,2048]{1,0:T(8,128)(2,1)S(1)}, bf16[128,2048]{1,0:T(8,128)(2,1)S(1)}, u32[]{:S(2)}, u32[]{:S(2)}) collective-permute-start(bf16[128,2048]{1,0:T(8,128)(2,1)S(1)} %add_share.22), channel_id=1, source_target_pairs={{0,8},{8,16},{16,24},{1,9},{9,17},{17,25},{2,10},{10,18},{18,26},{... | collective-permute-start | bytes 1572872 | tf_op jit(solution)/shard_map/ppermute | solution.py:255
  99.5 7.5 %weight_product.1 = bf16[1024,2048]{1,0:T(8,128)(2,1)} custom-call(bf16[1024,1024]{1,0:T(8,128)(2,1)S(1)} %lay_strips.1.refs_1_.cot_ref, bf16[256,2048]{1,0:T(8,128)(2,1)S(1)} %pad_maximum_fusion.own_ref, bf16[128,2048]{1,0:T(8,128)(2,1)S(1)} %collective-permute-done.9.refs_0_, bf16[128,2048]{1,0:T(8,128)(2,1)S(1)} %collective-permute-done.16.refs_0_.refs_1_, ...), custom_call_target="tpu_custom_call" | custom-call | flops 4294967296 | bytes 8388608 | tf_op jit(solution)/shard_map/weight_product/pallas_call | solution.py:128
  108.4 8.5 %collective-permute-done.26.refs_4_ = bf16[128,2048]{1,0:T(8,128)(2,1)S(1)} collective-permute-done((bf16[128,2048]{1,0:T(8,128)(2,1)S(1)}, bf16[128,2048]{1,0:T(8,128)(2,1)S(1)}, u32[]{:S(2)}, u32[]{:S(2)}) %collective-permute-start.26) | collective-permute-done | bytes 524320 | tf_op jit(solution)/shard_map/ppermute | solution.py:255
  (64 shorter events, 26.3 us)
Async XLA Ops:
  1.6 6.8 %collective-permute-start = (bf16[64,512]{1,0:T(8,128)(2,1)S(1)}, bf16[64,512]{1,0:T(8,128)(2,1)S(1)}, u32[]{:S(2)}, u32[]{:S(2)}) collective-permute-start(bf16[64,512]{1,0:T(8,128)(2,1)S(1)} %get-tuple-element.60), channel_id=1, source_target_pairs={{0,2},{1,3},{2,0},{3,1},{4,6},{5,7},{6,4},{7,5},{8,10},{9,11},{10,... | collective-permute-start | bytes 196616 | tf_op jit(solution)/shard_map/ppermute | solution.py:183
  11.4 10.3 %collective-permute-start.3 = (bf16[64,512]{1,0:T(8,128)(2,1)S(1)}, bf16[64,512]{1,0:T(8,128)(2,1)S(1)}, u32[]{:S(2)}, u32[]{:S(2)}) collective-permute-start(bf16[64,512]{1,0:T(8,128)(2,1)S(1)} %get-tuple-element.58), channel_id=1, source_target_pairs={{0,8},{8,0},{16,24},{24,16},{1,9},{9,1},{17,25},{25,17},{2,10},{10... | collective-permute-start | bytes 196616 | tf_op jit(solution)/shard_map/ppermute | solution.py:213
  13.0 8.7 %collective-permute-start.4 = (bf16[64,512]{1,0:T(8,128)(2,1)S(1)}, bf16[64,512]{1,0:T(8,128)(2,1)S(1)}, u32[]{:S(2)}, u32[]{:S(2)}) collective-permute-start(bf16[64,512]{1,0:T(8,128)(2,1)S(1)} %get-tuple-element.57), channel_id=1, source_target_pairs={{0,16},{8,24},{16,0},{24,8},{1,17},{9,25},{17,1},{25,9},{2,18},{10... | collective-permute-start | bytes 196616 | tf_op jit(solution)/shard_map/ppermute | solution.py:213
  15.6 6.8 %collective-permute-start.5 = (bf16[64,512]{1,0:T(8,128)(2,1)S(1)}, bf16[64,512]{1,0:T(8,128)(2,1)S(1)}, u32[]{:S(2)}, u32[]{:S(2)}) collective-permute-start(bf16[64,512]{1,0:T(8,128)(2,1)S(1)} %get-tuple-element.56), channel_id=1, source_target_pairs={{0,24},{8,16},{16,8},{24,0},{1,25},{9,17},{17,9},{25,1},{2,26},{10... | collective-permute-start | bytes 196616 | tf_op jit(solution)/shard_map/ppermute | solution.py:213
  15.9 20.8 %collective-permute-start.10 = (bf16[128,2048]{1,0:T(8,128)(2,1)S(1)}, bf16[128,2048]{1,0:T(8,128)(2,1)S(1)}, u32[]{:S(2)}, u32[]{:S(2)}) collective-permute-start(bf16[128,2048]{1,0:T(8,128)(2,1)S(1)} %get-tuple-element.54), channel_id=1, source_target_pairs={{8,0},{16,8},{24,16},{9,1},{17,9},{25,17},{10,2},{18,10},{26,18},{... | collective-permute-start | bytes 1572872 | tf_op jit(solution)/shard_map/ppermute | solution.py:238
  17.1 19.6 %collective-permute-start.9 = (bf16[128,2048]{1,0:T(8,128)(2,1)S(1)}, bf16[128,2048]{1,0:T(8,128)(2,1)S(1)}, u32[]{:S(2)}, u32[]{:S(2)}) collective-permute-start(bf16[128,2048]{1,0:T(8,128)(2,1)S(1)} %get-tuple-element.54), channel_id=1, source_target_pairs={{0,8},{8,16},{16,24},{1,9},{9,17},{17,25},{2,10},{10,18},{18,26},{... | collective-permute-start | bytes 1572872 | tf_op jit(solution)/shard_map/ppermute | solution.py:237
  22.5 8.4 %collective-permute-start.8 = (bf16[4,64,512]{2,1,0:T(8,128)(2,1)S(1)}, bf16[4,64,512]{2,1,0:T(8,128)(2,1)S(1)}, u32[]{:S(2)}, u32[]{:S(2)}) collective-permute-start(bf16[4,64,512]{2,1,0:T(8,128)(2,1)S(1)} %pad_maximum_fusion.2.refs_0_), channel_id=1, source_target_pairs={{0,6},{1,7},{2,4},{3,5},{4,2},{5,3},{6,0},{7,1},{8,14},{9,15},{10,... | collective-permute-start | bytes 786440 | tf_op jit(solution)/shard_map/ppermute | solution.py:183
  23.1 9.6 %collective-permute-start.6 = (bf16[4,64,512]{2,1,0:T(8,128)(2,1)S(1)}, bf16[4,64,512]{2,1,0:T(8,128)(2,1)S(1)}, u32[]{:S(2)}, u32[]{:S(2)}) collective-permute-start(bf16[4,64,512]{2,1,0:T(8,128)(2,1)S(1)} %pad_maximum_fusion.2.refs_0_), channel_id=1, source_target_pairs={{0,2},{1,3},{2,0},{3,1},{4,6},{5,7},{6,4},{7,5},{8,10},{9,11},{10,... | collective-permute-start | bytes 786440 | tf_op jit(solution)/shard_map/ppermute | solution.py:183
  24.5 10.8 %collective-permute-start.7 = (bf16[4,64,512]{2,1,0:T(8,128)(2,1)S(1)}, bf16[4,64,512]{2,1,0:T(8,128)(2,1)S(1)}, u32[]{:S(2)}, u32[]{:S(2)}) collective-permute-start(bf16[4,64,512]{2,1,0:T(8,128)(2,1)S(1)} %pad_maximum_fusion.2.refs_0_), channel_id=1, source_target_pairs={{0,4},{1,5},{2,6},{3,7},{4,0},{5,1},{6,2},{7,3},{8,12},{9,13},{10,... | collective-permute-start | bytes 786440 | tf_op jit(solution)/shard_map/ppermute | solution.py:183
  30.9 6.3 %collective-permute-start.11 = (bf16[4,64,512]{2,1,0:T(8,128)(2,1)S(1)}, bf16[4,64,512]{2,1,0:T(8,128)(2,1)S(1)}, u32[]{:S(2)}, u32[]{:S(2)}) collective-permute-start(bf16[4,64,512]{2,1,0:T(8,128)(2,1)S(1)} %pad_maximum_fusion.2.refs_0_), channel_id=1, source_target_pairs={{0,1},{1,0},{2,3},{3,2},{4,5},{5,4},{6,7},{7,6},{8,9},{9,8},{10,11... | collective-permute-start | bytes 786440 | tf_op jit(solution)/shard_map/ppermute | solution.py:183
  32.7 13.9 %collective-permute-start.16 = (bf16[128,2048]{1,0:T(8,128)(2,1)S(1)}, bf16[128,2048]{1,0:T(8,128)(2,1)S(1)}, u32[]{:S(2)}, u32[]{:S(2)}) collective-permute-start(bf16[128,2048]{1,0:T(8,128)(2,1)S(1)} %get-tuple-element.53), channel_id=1, source_target_pairs={{0,8},{8,16},{16,24},{1,9},{9,17},{17,25},{2,10},{10,18},{18,26},{... | collective-permute-start | bytes 1572872 | tf_op jit(solution)/shard_map/ppermute | solution.py:237
  35.3 15.7 %collective-permute-start.15 = (bf16[128,2048]{1,0:T(8,128)(2,1)S(1)}, bf16[128,2048]{1,0:T(8,128)(2,1)S(1)}, u32[]{:S(2)}, u32[]{:S(2)}) collective-permute-start(bf16[128,2048]{1,0:T(8,128)(2,1)S(1)} %get-tuple-element.53), channel_id=1, source_target_pairs={{8,0},{16,8},{24,16},{9,1},{17,9},{25,17},{10,2},{18,10},{26,18},{... | collective-permute-start | bytes 1572872 | tf_op jit(solution)/shard_map/ppermute | solution.py:238
  39.9 17.9 %collective-permute-start.20 = (bf16[128,2048]{1,0:T(8,128)(2,1)S(1)}, bf16[128,2048]{1,0:T(8,128)(2,1)S(1)}, u32[]{:S(2)}, u32[]{:S(2)}) collective-permute-start(bf16[128,2048]{1,0:T(8,128)(2,1)S(1)} %add_share.12), channel_id=1, source_target_pairs={{0,8},{8,16},{16,24},{1,9},{9,17},{17,25},{2,10},{10,18},{18,26},{... | collective-permute-start | bytes 1572872 | tf_op jit(solution)/shard_map/ppermute | solution.py:255
  43.9 19.1 %collective-permute-start.19 = (bf16[128,2048]{1,0:T(8,128)(2,1)S(1)}, bf16[128,2048]{1,0:T(8,128)(2,1)S(1)}, u32[]{:S(2)}, u32[]{:S(2)}) collective-permute-start(bf16[128,2048]{1,0:T(8,128)(2,1)S(1)} %add_share.13), channel_id=1, source_target_pairs={{8,0},{16,8},{24,16},{9,1},{17,9},{25,17},{10,2},{18,10},{26,18},{... | collective-permute-start | bytes 1572872 | tf_op jit(solution)/shard_map/ppermute | solution.py:255
  47.3 21.7 %collective-permute-start.18 = (bf16[128,2048]{1,0:T(8,128)(2,1)S(1)}, bf16[128,2048]{1,0:T(8,128)(2,1)S(1)}, u32[]{:S(2)}, u32[]{:S(2)}) collective-permute-start(bf16[128,2048]{1,0:T(8,128)(2,1)S(1)} %add_share.14), channel_id=1, source_target_pairs={{0,8},{8,16},{16,24},{1,9},{9,17},{17,25},{2,10},{10,18},{18,26},{... | collective-permute-start | bytes 1572872 | tf_op jit(solution)/shard_map/ppermute | solution.py:255
  51.1 23.1 %collective-permute-start.17 = (bf16[128,2048]{1,0:T(8,128)(2,1)S(1)}, bf16[128,2048]{1,0:T(8,128)(2,1)S(1)}, u32[]{:S(2)}, u32[]{:S(2)}) collective-permute-start(bf16[128,2048]{1,0:T(8,128)(2,1)S(1)} %add_share.15), channel_id=1, source_target_pairs={{8,0},{16,8},{24,16},{9,1},{17,9},{25,17},{10,2},{18,10},{26,18},{... | collective-permute-start | bytes 1572872 | tf_op jit(solution)/shard_map/ppermute | solution.py:255
  58.5 21.7 %collective-permute-start.24 = (bf16[128,2048]{1,0:T(8,128)(2,1)S(1)}, bf16[128,2048]{1,0:T(8,128)(2,1)S(1)}, u32[]{:S(2)}, u32[]{:S(2)}) collective-permute-start(bf16[128,2048]{1,0:T(8,128)(2,1)S(1)} %add_share.16), channel_id=1, source_target_pairs={{0,8},{8,16},{16,24},{1,9},{9,17},{17,25},{2,10},{10,18},{18,26},{... | collective-permute-start | bytes 1572872 | tf_op jit(solution)/shard_map/ppermute | solution.py:255
  63.0 22.4 %collective-permute-start.23 = (bf16[128,2048]{1,0:T(8,128)(2,1)S(1)}, bf16[128,2048]{1,0:T(8,128)(2,1)S(1)}, u32[]{:S(2)}, u32[]{:S(2)}) collective-permute-start(bf16[128,2048]{1,0:T(8,128)(2,1)S(1)} %add_share.17), channel_id=1, source_target_pairs={{8,0},{16,8},{24,16},{9,1},{17,9},{25,17},{10,2},{18,10},{26,18},{... | collective-permute-start | bytes 1572872 | tf_op jit(solution)/shard_map/ppermute | solution.py:255
  69.8 21.7 %collective-permute-start.22 = (bf16[128,2048]{1,0:T(8,128)(2,1)S(1)}, bf16[128,2048]{1,0:T(8,128)(2,1)S(1)}, u32[]{:S(2)}, u32[]{:S(2)}) collective-permute-start(bf16[128,2048]{1,0:T(8,128)(2,1)S(1)} %add_share.18), channel_id=1, source_target_pairs={{0,8},{8,16},{16,24},{1,9},{9,17},{17,25},{2,10},{10,18},{18,26},{... | collective-permute-start | bytes 1572872 | tf_op jit(solution)/shard_map/ppermute | solution.py:255
  74.3 22.4 %collective-permute-start.21 = (bf16[128,2048]{1,0:T(8,128)(2,1)S(1)}, bf16[128,2048]{1,0:T(8,128)(2,1)S(1)}, u32[]{:S(2)}, u32[]{:S(2)}) collective-permute-start(bf16[128,2048]{1,0:T(8,128)(2,1)S(1)} %add_share.19), channel_id=1, source_target_pairs={{8,0},{16,8},{24,16},{9,1},{17,9},{25,17},{10,2},{18,10},{26,18},{... | collective-permute-start | bytes 1572872 | tf_op jit(solution)/shard_map/ppermute | solution.py:255
  81.0 26.0 %collective-permute-start.27 = (bf16[128,2048]{1,0:T(8,128)(2,1)S(1)}, bf16[128,2048]{1,0:T(8,128)(2,1)S(1)}, u32[]{:S(2)}, u32[]{:S(2)}) collective-permute-start(bf16[128,2048]{1,0:T(8,128)(2,1)S(1)} %add_share.20), channel_id=1, source_target_pairs={{0,8},{8,16},{16,24},{1,9},{9,17},{17,25},{2,10},{10,18},{18,26},{... | collective-permute-start | bytes 1572872 | tf_op jit(solution)/shard_map/ppermute | solution.py:255
  85.5 21.5 %collective-permute-start.28 = (bf16[128,2048]{1,0:T(8,128)(2,1)S(1)}, bf16[128,2048]{1,0:T(8,128)(2,1)S(1)}, u32[]{:S(2)}, u32[]{:S(2)}) collective-permute-start(bf16[128,2048]{1,0:T(8,128)(2,1)S(1)} %add_share.21), channel_id=1, source_target_pairs={{8,0},{16,8},{24,16},{9,1},{17,9},{25,17},{10,2},{18,10},{26,18},{... | collective-permute-start | bytes 1572872 | tf_op jit(solution)/shard_map/ppermute | solution.py:255
  92.2 24.7 %collective-permute-start.25 = (bf16[128,2048]{1,0:T(8,128)(2,1)S(1)}, bf16[128,2048]{1,0:T(8,128)(2,1)S(1)}, u32[]{:S(2)}, u32[]{:S(2)}) collective-permute-start(bf16[128,2048]{1,0:T(8,128)(2,1)S(1)} %add_share.22), channel_id=1, source_target_pairs={{0,8},{8,16},{16,24},{1,9},{9,17},{17,25},{2,10},{10,18},{18,26},{... | collective-permute-start | bytes 1572872 | tf_op jit(solution)/shard_map/ppermute | solution.py:255
  96.7 20.2 %collective-permute-start.26 = (bf16[128,2048]{1,0:T(8,128)(2,1)S(1)}, bf16[128,2048]{1,0:T(8,128)(2,1)S(1)}, u32[]{:S(2)}, u32[]{:S(2)}) collective-permute-start(bf16[128,2048]{1,0:T(8,128)(2,1)S(1)} %add_share.23), channel_id=1, source_target_pairs={{8,0},{16,8},{24,16},{9,1},{17,9},{25,17},{10,2},{18,10},{26,18},{... | collective-permute-start | bytes 1572872 | tf_op jit(solution)/shard_map/ppermute | solution.py:255
  (8 other events, 36.3 us)
where the time goes:
time: 119 us; the launch traced here: 118 us
  starting transfers between devices  56.1 us (47%)
  waiting for transfers between devices  41.2 us (35%)
  Pallas kernels  15.2 us (13%)
  other arithmetic  2.33 us (2%)
  between operations  1.28 us (1%)
  matrix products  1.25 us (1%)
    ppermute x12, starting transfers between devices, per_device(): ends[step][at] = lax.ppermute(turn, 'row', pairs)  33.2 us
    ppermute x12, waiting for transfers between devices, per_device(): ends[step][at] = lax.ppermute(turn, 'row', pairs)  27.9 us
    ppermute x10, waiting for transfers between devices, swap(): lax.ppermute(value, 'col', [(at, at ^ bits) for at in range(lax.axis_size...  11.2 us
    ppermute x10, starting transfers between devices, swap(): lax.ppermute(value, 'col', [(at, at ^ bits) for at in range(lax.axis_size...  8.75 us
    pallas_call x1, Pallas kernels, weight_product(): pl.pallas_call(kernel, out_shape=jax.ShapeDtypeStruct((cot.shape[1], widt...  7.53 us
    ppermute x2, starting transfers between devices, per_device(): fore[1].append(lax.ppermute(hidden[-1].astype(wire), 'row', ahead))  7.17 us
    pallas_call x12, Pallas kernels, add_share(): pl.pallas_call(kernel, out_shape=jax.ShapeDtypeStruct((span, width), like...  4.71 us
    ppermute x3, starting transfers between devices, across(): lax.ppermute(piece, 'row', [(at, at ^ bits) for at in range(rows)])  4.45 us
  transfers between devices with their start and end apart: 29, of which 14 were waited for; matrix products, arithmetic and copies ran while one was open for 3% of the time, Pallas kernels for 12%

commit v1 on v0

--- a/solution.py
+++ b/solution.py
@@ -201,21 +201,21 @@
         return blocks.transpose(0, 2, 1, 3).reshape(rows * tok_rows, per_row * width)
     strip = tok_rows * 2 // cols
     chip = lax.axis_index("col") // 2
+    grad_out = after(grad_out, hidden[0])
 
     def quarter(bits):
         piece = lax.dynamic_slice_in_dim(grad_out, (chip ^ bits) * strip, strip, 0)
         return swap(piece, 2 * bits) if bits else piece
 
-    wide = after([quarter(bits) for bits in range(cols // 2)], hidden[0])
+    wide = [quarter(bits) for bits in range(cols // 2)]
 
     def across(bits):
         piece = lax.dynamic_index_in_dim(jnp.stack(wide), chip ^ row ^ bits, 0, keepdims=False)
         return lax.ppermute(piece, "row", [(at, at ^ bits) for at in range(rows)]) if bits else piece
 
     tall = [across(bits) for bits in range(rows - 1, -1, -1)]
-    tall = jnp.stack(tall[::-1])
+    tall = after(jnp.stack(tall[::-1]), first)
     near = [tall, swap(tall, 2), swap(tall, 4), swap(tall, 6)]
-    near[-1] = after(near[-1], first)
     return lay_strips(near, [swap(block, 1) for block in near])
 
 

time: 119 us -> 122 us (1.025)
  waiting for transfers between devices: 41.2 us -> 46.5 us
  starting transfers between devices: 56.1 us -> 54.4 us
    ppermute x3, waiting for transfers between devices: 0.71 us -> 6.59 us  [across(): lax.ppermute(piece, 'row', [(at, at ^ bits) for at in range(rows)])]
    ppermute x12, starting transfers between devices: 33.2 us -> 30.8 us  [per_device(): ends[step][at] = lax.ppermute(turn, 'row', pairs)]
    ppermute x2, waiting for transfers between devices: 1.39 us -> 0.01 us  [per_device(): fore[1].append(lax.ppermute(hidden[-1].astype(wire), 'row', ahead))]
  transfers between devices with their start and end apart: 29 -> 29, of which waited for: 14 -> 17; matrix products, arithmetic and copies ran while one was open for 3% -> 1% of each run, Pallas kernels for 12% -> 11%
where the time goes in v1:
time: 122 us; the launch traced here: 121 us
  starting transfers between devices  54.4 us (45%)
  waiting for transfers between devices  46.5 us (38%)
  Pallas kernels  15.2 us (12%)
  other arithmetic  2.37 us (2%)
  matrix products  1.25 us (1%)
  between operations  1.24 us (1%)
    ppermute x12, starting transfers between devices, per_device(): ends[step][at] = lax.ppermute(turn, 'row', pairs)  30.8 us
    ppermute x12, waiting for transfers between devices, per_device(): ends[step][at] = lax.ppermute(turn, 'row', pairs)  28.1 us
    ppermute x10, waiting for transfers between devices, swap(): lax.ppermute(value, 'col', [(at, at ^ bits) for at in range(lax.axis_size...  11.8 us
    ppermute x2, starting transfers between devices, per_device(): fore[1].append(lax.ppermute(hidden[-1].astype(wire), 'row', ahead))  8 us
    ppermute x10, starting transfers between devices, swap(): lax.ppermute(value, 'col', [(at, at ^ bits) for at in range(lax.axis_size...  7.69 us
    pallas_call x1, Pallas kernels, weight_product(): pl.pallas_call(kernel, out_shape=jax.ShapeDtypeStruct((cot.shape[1], widt...  7.53 us
    ppermute x3, waiting for transfers between devices, across(): lax.ppermute(piece, 'row', [(at, at ^ bits) for at in range(rows)])  6.59 us
    ppermute x3, starting transfers between devices, across(): lax.ppermute(piece, 'row', [(at, at ^ bits) for at in range(rows)])  5.3 us
  transfers between devices with their start and end apart: 29, of which 17 were waited for; matrix products, arithmetic and copies ran while one was open for 1% of the time, Pallas kernels for 11%

profile of v1, /device:TPU:0, one launch (start us, length us, event | category | flops | bytes accessed | tf_op | source)
XLA Modules:
  0.0 121.1 jit_solution(14270187090260816057)
XLA Ops:
  0.6 2.2 %fusion.8 = (bf16[128,2048]{1,0:T(8,128)(2,1)S(1)}, bf16[128,2048]{1,0:T(8,128)(2,1)S(1)}) fusion(bf16[256,2048]{1,0:T(8,128)(2,1)} %refs_1_.1, bf16[256,2048]{1,0:T(8,128)(2,1)} %refs_0_.1), kind=kLoop, calls=%fused_computation.13 | loop fusion | flops 4194304 | bytes 3145728 | tf_op jit(solution)/shard_map/convert_element_type | solution.py:236
  2.9 5.0 %collective-permute-start.6 = (bf16[128,2048]{1,0:T(8,128)(2,1)S(1)}, bf16[128,2048]{1,0:T(8,128)(2,1)S(1)}, u32[]{:S(2)}, u32[]{:S(2)}) collective-permute-start(bf16[128,2048]{1,0:T(8,128)(2,1)S(1)} %get-tuple-element.48), channel_id=1, source_target_pairs={{0,8},{8,16},{16,24},{1,9},{9,17},{17,25},{2,10},{10,18},{18,26},{... | collective-permute-start | bytes 1572872 | tf_op jit(solution)/shard_map/ppermute | solution.py:237
  9.2 1.6 %collective-permute-start = (bf16[64,512]{1,0:T(8,128)(2,1)S(1)}, bf16[64,512]{1,0:T(8,128)(2,1)S(1)}, u32[]{:S(2)}, u32[]{:S(2)}) collective-permute-start(bf16[64,512]{1,0:T(8,128)(2,1)S(1)} %get-tuple-element.56), channel_id=1, source_target_pairs={{0,2},{1,3},{2,0},{3,1},{4,6},{5,7},{6,4},{7,5},{8,10},{9,11},{10,... | collective-permute-start | bytes 196616 | tf_op jit(solution)/shard_map/ppermute | solution.py:183
  13.6 2.2 %collective-permute-done.1 = bf16[64,512]{1,0:T(8,128)(2,1)S(1)} collective-permute-done((bf16[64,512]{1,0:T(8,128)(2,1)S(1)}, bf16[64,512]{1,0:T(8,128)(2,1)S(1)}, u32[]{:S(2)}, u32[]{:S(2)}) %collective-permute-start.1) | collective-permute-done | bytes 65568 | tf_op jit(solution)/shard_map/ppermute | solution.py:183
  15.8 1.7 %collective-permute-done.2 = bf16[64,512]{1,0:T(8,128)(2,1)S(1)} collective-permute-done((bf16[64,512]{1,0:T(8,128)(2,1)S(1)}, bf16[64,512]{1,0:T(8,128)(2,1)S(1)}, u32[]{:S(2)}, u32[]{:S(2)}) %collective-permute-start.2) | collective-permute-done | bytes 65568 | tf_op jit(solution)/shard_map/ppermute | solution.py:183
  17.5 2.7 %collective-permute-start.3 = (bf16[64,512]{1,0:T(8,128)(2,1)S(1)}, bf16[64,512]{1,0:T(8,128)(2,1)S(1)}, u32[]{:S(2)}, u32[]{:S(2)}) collective-permute-start(bf16[64,512]{1,0:T(8,128)(2,1)S(1)} %get-tuple-element.52), channel_id=1, source_target_pairs={{0,8},{8,0},{16,24},{24,16},{1,9},{9,1},{17,25},{25,17},{2,10},{10... | collective-permute-start | bytes 196616 | tf_op jit(solution)/shard_map/ppermute | solution.py:214
  20.3 2.6 %collective-permute-start.4 = (bf16[64,512]{1,0:T(8,128)(2,1)S(1)}, bf16[64,512]{1,0:T(8,128)(2,1)S(1)}, u32[]{:S(2)}, u32[]{:S(2)}) collective-permute-start(bf16[64,512]{1,0:T(8,128)(2,1)S(1)} %get-tuple-element.51), channel_id=1, source_target_pairs={{0,16},{8,24},{16,0},{24,8},{1,17},{9,25},{17,1},{25,9},{2,18},{10... | collective-permute-start | bytes 196616 | tf_op jit(solution)/shard_map/ppermute | solution.py:214
  22.8 2.4 %collective-permute-done.3 = bf16[64,512]{1,0:T(8,128)(2,1)S(1)} collective-permute-done((bf16[64,512]{1,0:T(8,128)(2,1)S(1)}, bf16[64,512]{1,0:T(8,128)(2,1)S(1)}, u32[]{:S(2)}, u32[]{:S(2)}) %collective-permute-start.3) | collective-permute-done | bytes 65568 | tf_op jit(solution)/shard_map/ppermute | solution.py:214
  25.2 2.1 %collective-permute-done.4 = bf16[64,512]{1,0:T(8,128)(2,1)S(1)} collective-permute-done((bf16[64,512]{1,0:T(8,128)(2,1)S(1)}, bf16[64,512]{1,0:T(8,128)(2,1)S(1)}, u32[]{:S(2)}, u32[]{:S(2)}) %collective-permute-start.4) | collective-permute-done | bytes 65568 | tf_op jit(solution)/shard_map/ppermute | solution.py:214
  27.4 2.1 %collective-permute-done.5 = bf16[64,512]{1,0:T(8,128)(2,1)S(1)} collective-permute-done((bf16[64,512]{1,0:T(8,128)(2,1)S(1)}, bf16[64,512]{1,0:T(8,128)(2,1)S(1)}, u32[]{:S(2)}, u32[]{:S(2)}) %collective-permute-start.5) | collective-permute-done | bytes 65568 | tf_op jit(solution)/shard_map/ppermute | solution.py:214
  33.1 3.0 %collective-permute-start.16 = (bf16[128,2048]{1,0:T(8,128)(2,1)S(1)}, bf16[128,2048]{1,0:T(8,128)(2,1)S(1)}, u32[]{:S(2)}, u32[]{:S(2)}) collective-permute-start(bf16[128,2048]{1,0:T(8,128)(2,1)S(1)} %get-tuple-element.47), channel_id=1, source_target_pairs={{0,8},{8,16},{16,24},{1,9},{9,17},{17,25},{2,10},{10,18},{18,26},{... | collective-permute-start | bytes 1572872 | tf_op jit(solution)/shard_map/ppermute | solution.py:237
  36.1 2.7 %collective-permute-done.8.refs_1_ = bf16[4,64,512]{2,1,0:T(8,128)(2,1)S(1)} collective-permute-done((bf16[4,64,512]{2,1,0:T(8,128)(2,1)S(1)}, bf16[4,64,512]{2,1,0:T(8,128)(2,1)S(1)}, u32[]{:S(2)}, u32[]{:S(2)}) %collective-permute-start.8) | collective-permute-done | bytes 262176 | tf_op jit(solution)/shard_map/ppermute | solution.py:183
  40.1 2.8 %collective-permute-done.9.refs_2_ = bf16[4,64,512]{2,1,0:T(8,128)(2,1)S(1)} collective-permute-done((bf16[4,64,512]{2,1,0:T(8,128)(2,1)S(1)}, bf16[4,64,512]{2,1,0:T(8,128)(2,1)S(1)}, u32[]{:S(2)}, u32[]{:S(2)}) %collective-permute-start.9) | collective-permute-done | bytes 262176 | tf_op jit(solution)/shard_map/ppermute | solution.py:183
  49.5 3.9 %collective-permute-start.18 = (bf16[128,2048]{1,0:T(8,128)(2,1)S(1)}, bf16[128,2048]{1,0:T(8,128)(2,1)S(1)}, u32[]{:S(2)}, u32[]{:S(2)}) collective-permute-start(bf16[128,2048]{1,0:T(8,128)(2,1)S(1)} %add_share.14), channel_id=1, source_target_pairs={{0,8},{8,16},{16,24},{1,9},{9,17},{17,25},{2,10},{10,18},{18,26},{... | collective-permute-start | bytes 1572872 | tf_op jit(solution)/shard_map/ppermute | solution.py:255
  54.8 4.8 %collective-permute-done.20.refs_0_.refs_2_ = bf16[128,2048]{1,0:T(8,128)(2,1)S(1)} collective-permute-done((bf16[128,2048]{1,0:T(8,128)(2,1)S(1)}, bf16[128,2048]{1,0:T(8,128)(2,1)S(1)}, u32[]{:S(2)}, u32[]{:S(2)}) %collective-permute-start.20) | collective-permute-done | bytes 524320 | tf_op jit(solution)/shard_map/ppermute | solution.py:255
  60.3 4.4 %collective-permute-start.24 = (bf16[128,2048]{1,0:T(8,128)(2,1)S(1)}, bf16[128,2048]{1,0:T(8,128)(2,1)S(1)}, u32[]{:S(2)}, u32[]{:S(2)}) collective-permute-start(bf16[128,2048]{1,0:T(8,128)(2,1)S(1)} %add_share.16), channel_id=1, source_target_pairs={{0,8},{8,16},{16,24},{1,9},{9,17},{17,25},{2,10},{10,18},{18,26},{... | collective-permute-start | bytes 1572872 | tf_op jit(solution)/shard_map/ppermute | solution.py:255
  66.1 4.7 %collective-permute-done.18.refs_0_.refs_3_ = bf16[128,2048]{1,0:T(8,128)(2,1)S(1)} collective-permute-done((bf16[128,2048]{1,0:T(8,128)(2,1)S(1)}, bf16[128,2048]{1,0:T(8,128)(2,1)S(1)}, u32[]{:S(2)}, u32[]{:S(2)}) %collective-permute-start.18) | collective-permute-done | bytes 524320 | tf_op jit(solution)/shard_map/ppermute | solution.py:255
  71.6 4.4 %collective-permute-start.22 = (bf16[128,2048]{1,0:T(8,128)(2,1)S(1)}, bf16[128,2048]{1,0:T(8,128)(2,1)S(1)}, u32[]{:S(2)}, u32[]{:S(2)}) collective-permute-start(bf16[128,2048]{1,0:T(8,128)(2,1)S(1)} %add_share.18), channel_id=1, source_target_pairs={{0,8},{8,16},{16,24},{1,9},{9,17},{17,25},{2,10},{10,18},{18,26},{... | collective-permute-start | bytes 1572872 | tf_op jit(solution)/shard_map/ppermute | solution.py:255
  77.5 4.6 %collective-permute-done.24.refs_0_.refs_4_ = bf16[128,2048]{1,0:T(8,128)(2,1)S(1)} collective-permute-done((bf16[128,2048]{1,0:T(8,128)(2,1)S(1)}, bf16[128,2048]{1,0:T(8,128)(2,1)S(1)}, u32[]{:S(2)}, u32[]{:S(2)}) %collective-permute-start.24) | collective-permute-done | bytes 524320 | tf_op jit(solution)/shard_map/ppermute | solution.py:255
  82.8 4.4 %collective-permute-start.27 = (bf16[128,2048]{1,0:T(8,128)(2,1)S(1)}, bf16[128,2048]{1,0:T(8,128)(2,1)S(1)}, u32[]{:S(2)}, u32[]{:S(2)}) collective-permute-start(bf16[128,2048]{1,0:T(8,128)(2,1)S(1)} %add_share.20), channel_id=1, source_target_pairs={{0,8},{8,16},{16,24},{1,9},{9,17},{17,25},{2,10},{10,18},{18,26},{... | collective-permute-start | bytes 1572872 | tf_op jit(solution)/shard_map/ppermute | solution.py:255
  88.6 4.7 %collective-permute-done.22.refs_0_.refs_5_ = bf16[128,2048]{1,0:T(8,128)(2,1)S(1)} collective-permute-done((bf16[128,2048]{1,0:T(8,128)(2,1)S(1)}, bf16[128,2048]{1,0:T(8,128)(2,1)S(1)}, u32[]{:S(2)}, u32[]{:S(2)}) %collective-permute-start.22) | collective-permute-done | bytes 524320 | tf_op jit(solution)/shard_map/ppermute | solution.py:255
  94.0 4.4 %collective-permute-start.25 = (bf16[128,2048]{1,0:T(8,128)(2,1)S(1)}, bf16[128,2048]{1,0:T(8,128)(2,1)S(1)}, u32[]{:S(2)}, u32[]{:S(2)}) collective-permute-start(bf16[128,2048]{1,0:T(8,128)(2,1)S(1)} %add_share.22), channel_id=1, source_target_pairs={{0,8},{8,16},{16,24},{1,9},{9,17},{17,25},{2,10},{10,18},{18,26},{... | collective-permute-start | bytes 1572872 | tf_op jit(solution)/shard_map/ppermute | solution.py:255
  101.3 7.5 %weight_product.1 = bf16[1024,2048]{1,0:T(8,128)(2,1)} custom-call(bf16[1024,1024]{1,0:T(8,128)(2,1)S(1)} %lay_strips.1.refs_1_.cot_ref, bf16[256,2048]{1,0:T(8,128)(2,1)S(1)} %pad_maximum_fusion.own_ref, bf16[128,2048]{1,0:T(8,128)(2,1)S(1)} %collective-permute-done.6.refs_0_, bf16[128,2048]{1,0:T(8,128)(2,1)S(1)} %collective-permute-done.16.refs_0_.refs_1_, ...), custom_call_target="tpu_custom_call" | custom-call | flops 4294967296 | bytes 8388608 | tf_op jit(solution)/shard_map/weight_product/pallas_call | solution.py:128
  110.5 9.0 %collective-permute-done.26.refs_4_ = bf16[128,2048]{1,0:T(8,128)(2,1)S(1)} collective-permute-done((bf16[128,2048]{1,0:T(8,128)(2,1)S(1)}, bf16[128,2048]{1,0:T(8,128)(2,1)S(1)}, u32[]{:S(2)}, u32[]{:S(2)}) %collective-permute-start.26) | collective-permute-done | bytes 524320 | tf_op jit(solution)/shard_map/ppermute | solution.py:255
  (66 shorter events, 29.9 us)
Async XLA Ops:
  2.9 26.6 %collective-permute-start.6 = (bf16[128,2048]{1,0:T(8,128)(2,1)S(1)}, bf16[128,2048]{1,0:T(8,128)(2,1)S(1)}, u32[]{:S(2)}, u32[]{:S(2)}) collective-permute-start(bf16[128,2048]{1,0:T(8,128)(2,1)S(1)} %get-tuple-element.48), channel_id=1, source_target_pairs={{0,8},{8,16},{16,24},{1,9},{9,17},{17,25},{2,10},{10,18},{18,26},{... | collective-permute-start | bytes 1572872 | tf_op jit(solution)/shard_map/ppermute | solution.py:237
  7.8 21.6 %collective-permute-start.7 = (bf16[128,2048]{1,0:T(8,128)(2,1)S(1)}, bf16[128,2048]{1,0:T(8,128)(2,1)S(1)}, u32[]{:S(2)}, u32[]{:S(2)}) collective-permute-start(bf16[128,2048]{1,0:T(8,128)(2,1)S(1)} %get-tuple-element.48), channel_id=1, source_target_pairs={{8,0},{16,8},{24,16},{9,1},{17,9},{25,17},{10,2},{18,10},{26,18},{... | collective-permute-start | bytes 1572872 | tf_op jit(solution)/shard_map/ppermute | solution.py:238
  12.3 5.2 %collective-permute-start.2 = (bf16[64,512]{1,0:T(8,128)(2,1)S(1)}, bf16[64,512]{1,0:T(8,128)(2,1)S(1)}, u32[]{:S(2)}, u32[]{:S(2)}) collective-permute-start(bf16[64,512]{1,0:T(8,128)(2,1)S(1)} %get-tuple-element.54), channel_id=1, source_target_pairs={{0,6},{1,7},{2,4},{3,5},{4,2},{5,3},{6,0},{7,1},{8,14},{9,15},{10,... | collective-permute-start | bytes 196616 | tf_op jit(solution)/shard_map/ppermute | solution.py:183
  17.5 7.7 %collective-permute-start.3 = (bf16[64,512]{1,0:T(8,128)(2,1)S(1)}, bf16[64,512]{1,0:T(8,128)(2,1)S(1)}, u32[]{:S(2)}, u32[]{:S(2)}) collective-permute-start(bf16[64,512]{1,0:T(8,128)(2,1)S(1)} %get-tuple-element.52), channel_id=1, source_target_pairs={{0,8},{8,0},{16,24},{24,16},{1,9},{9,1},{17,25},{25,17},{2,10},{10... | collective-permute-start | bytes 196616 | tf_op jit(solution)/shard_map/ppermute | solution.py:214
  20.3 7.1 %collective-permute-start.4 = (bf16[64,512]{1,0:T(8,128)(2,1)S(1)}, bf16[64,512]{1,0:T(8,128)(2,1)S(1)}, u32[]{:S(2)}, u32[]{:S(2)}) collective-permute-start(bf16[64,512]{1,0:T(8,128)(2,1)S(1)} %get-tuple-element.51), channel_id=1, source_target_pairs={{0,16},{8,24},{16,0},{24,8},{1,17},{9,25},{17,1},{25,9},{2,18},{10... | collective-permute-start | bytes 196616 | tf_op jit(solution)/shard_map/ppermute | solution.py:214
  22.8 6.6 %collective-permute-start.5 = (bf16[64,512]{1,0:T(8,128)(2,1)S(1)}, bf16[64,512]{1,0:T(8,128)(2,1)S(1)}, u32[]{:S(2)}, u32[]{:S(2)}) collective-permute-start(bf16[64,512]{1,0:T(8,128)(2,1)S(1)} %get-tuple-element.50), channel_id=1, source_target_pairs={{0,24},{8,16},{16,8},{24,0},{1,25},{9,17},{17,9},{25,1},{2,26},{10... | collective-permute-start | bytes 196616 | tf_op jit(solution)/shard_map/ppermute | solution.py:214
  29.5 9.3 %collective-permute-start.8 = (bf16[4,64,512]{2,1,0:T(8,128)(2,1)S(1)}, bf16[4,64,512]{2,1,0:T(8,128)(2,1)S(1)}, u32[]{:S(2)}, u32[]{:S(2)}) collective-permute-start(bf16[4,64,512]{2,1,0:T(8,128)(2,1)S(1)} %pad_maximum_fusion.2.refs_0_), channel_id=1, source_target_pairs={{0,2},{1,3},{2,0},{3,1},{4,6},{5,7},{6,4},{7,5},{8,10},{9,11},{10,... | collective-permute-start | bytes 786440 | tf_op jit(solution)/shard_map/ppermute | solution.py:183
  31.1 11.8 %collective-permute-start.9 = (bf16[4,64,512]{2,1,0:T(8,128)(2,1)S(1)}, bf16[4,64,512]{2,1,0:T(8,128)(2,1)S(1)}, u32[]{:S(2)}, u32[]{:S(2)}) collective-permute-start(bf16[4,64,512]{2,1,0:T(8,128)(2,1)S(1)} %pad_maximum_fusion.2.refs_0_), channel_id=1, source_target_pairs={{0,4},{1,5},{2,6},{3,7},{4,0},{5,1},{6,2},{7,3},{8,12},{9,13},{10,... | collective-permute-start | bytes 786440 | tf_op jit(solution)/shard_map/ppermute | solution.py:183
  32.6 10.3 %collective-permute-start.10 = (bf16[4,64,512]{2,1,0:T(8,128)(2,1)S(1)}, bf16[4,64,512]{2,1,0:T(8,128)(2,1)S(1)}, u32[]{:S(2)}, u32[]{:S(2)}) collective-permute-start(bf16[4,64,512]{2,1,0:T(8,128)(2,1)S(1)} %pad_maximum_fusion.2.refs_0_), channel_id=1, source_target_pairs={{0,6},{1,7},{2,4},{3,5},{4,2},{5,3},{6,0},{7,1},{8,14},{9,15},{10,... | collective-permute-start | bytes 786440 | tf_op jit(solution)/shard_map/ppermute | solution.py:183
  33.1 10.3 %collective-permute-start.11 = (bf16[4,64,512]{2,1,0:T(8,128)(2,1)S(1)}, bf16[4,64,512]{2,1,0:T(8,128)(2,1)S(1)}, u32[]{:S(2)}, u32[]{:S(2)}) collective-permute-start(bf16[4,64,512]{2,1,0:T(8,128)(2,1)S(1)} %pad_maximum_fusion.2.refs_0_), channel_id=1, source_target_pairs={{0,1},{1,0},{2,3},{3,2},{4,5},{5,4},{6,7},{7,6},{8,9},{9,8},{10,11... | collective-permute-start | bytes 786440 | tf_op jit(solution)/shard_map/ppermute | solution.py:183
  33.1 15.7 %collective-permute-start.16 = (bf16[128,2048]{1,0:T(8,128)(2,1)S(1)}, bf16[128,2048]{1,0:T(8,128)(2,1)S(1)}, u32[]{:S(2)}, u32[]{:S(2)}) collective-permute-start(bf16[128,2048]{1,0:T(8,128)(2,1)S(1)} %get-tuple-element.47), channel_id=1, source_target_pairs={{0,8},{8,16},{16,24},{1,9},{9,17},{17,25},{2,10},{10,18},{18,26},{... | collective-permute-start | bytes 1572872 | tf_op jit(solution)/shard_map/ppermute | solution.py:237
  38.8 14.6 %collective-permute-start.15 = (bf16[128,2048]{1,0:T(8,128)(2,1)S(1)}, bf16[128,2048]{1,0:T(8,128)(2,1)S(1)}, u32[]{:S(2)}, u32[]{:S(2)}) collective-permute-start(bf16[128,2048]{1,0:T(8,128)(2,1)S(1)} %get-tuple-element.47), channel_id=1, source_target_pairs={{8,0},{16,8},{24,16},{9,1},{17,9},{25,17},{10,2},{18,10},{26,18},{... | collective-permute-start | bytes 1572872 | tf_op jit(solution)/shard_map/ppermute | solution.py:238
  46.1 13.5 %collective-permute-start.20 = (bf16[128,2048]{1,0:T(8,128)(2,1)S(1)}, bf16[128,2048]{1,0:T(8,128)(2,1)S(1)}, u32[]{:S(2)}, u32[]{:S(2)}) collective-permute-start(bf16[128,2048]{1,0:T(8,128)(2,1)S(1)} %add_share.12), channel_id=1, source_target_pairs={{0,8},{8,16},{16,24},{1,9},{9,17},{17,25},{2,10},{10,18},{18,26},{... | collective-permute-start | bytes 1572872 | tf_op jit(solution)/shard_map/ppermute | solution.py:255
  47.5 17.3 %collective-permute-start.19 = (bf16[128,2048]{1,0:T(8,128)(2,1)S(1)}, bf16[128,2048]{1,0:T(8,128)(2,1)S(1)}, u32[]{:S(2)}, u32[]{:S(2)}) collective-permute-start(bf16[128,2048]{1,0:T(8,128)(2,1)S(1)} %add_share.13), channel_id=1, source_target_pairs={{8,0},{16,8},{24,16},{9,1},{17,9},{25,17},{10,2},{18,10},{26,18},{... | collective-permute-start | bytes 1572872 | tf_op jit(solution)/shard_map/ppermute | solution.py:255
  49.5 21.3 %collective-permute-start.18 = (bf16[128,2048]{1,0:T(8,128)(2,1)S(1)}, bf16[128,2048]{1,0:T(8,128)(2,1)S(1)}, u32[]{:S(2)}, u32[]{:S(2)}) collective-permute-start(bf16[128,2048]{1,0:T(8,128)(2,1)S(1)} %add_share.14), channel_id=1, source_target_pairs={{0,8},{8,16},{16,24},{1,9},{9,17},{17,25},{2,10},{10,18},{18,26},{... | collective-permute-start | bytes 1572872 | tf_op jit(solution)/shard_map/ppermute | solution.py:255
  53.5 22.5 %collective-permute-start.17 = (bf16[128,2048]{1,0:T(8,128)(2,1)S(1)}, bf16[128,2048]{1,0:T(8,128)(2,1)S(1)}, u32[]{:S(2)}, u32[]{:S(2)}) collective-permute-start(bf16[128,2048]{1,0:T(8,128)(2,1)S(1)} %add_share.15), channel_id=1, source_target_pairs={{8,0},{16,8},{24,16},{9,1},{17,9},{25,17},{10,2},{18,10},{26,18},{... | collective-permute-start | bytes 1572872 | tf_op jit(solution)/shard_map/ppermute | solution.py:255
  60.3 21.7 %collective-permute-start.24 = (bf16[128,2048]{1,0:T(8,128)(2,1)S(1)}, bf16[128,2048]{1,0:T(8,128)(2,1)S(1)}, u32[]{:S(2)}, u32[]{:S(2)}) collective-permute-start(bf16[128,2048]{1,0:T(8,128)(2,1)S(1)} %add_share.16), channel_id=1, source_target_pairs={{0,8},{8,16},{16,24},{1,9},{9,17},{17,25},{2,10},{10,18},{18,26},{... | collective-permute-start | bytes 1572872 | tf_op jit(solution)/shard_map/ppermute | solution.py:255
  64.8 22.4 %collective-permute-start.23 = (bf16[128,2048]{1,0:T(8,128)(2,1)S(1)}, bf16[128,2048]{1,0:T(8,128)(2,1)S(1)}, u32[]{:S(2)}, u32[]{:S(2)}) collective-permute-start(bf16[128,2048]{1,0:T(8,128)(2,1)S(1)} %add_share.17), channel_id=1, source_target_pairs={{8,0},{16,8},{24,16},{9,1},{17,9},{25,17},{10,2},{18,10},{26,18},{... | collective-permute-start | bytes 1572872 | tf_op jit(solution)/shard_map/ppermute | solution.py:255
  71.6 21.7 %collective-permute-start.22 = (bf16[128,2048]{1,0:T(8,128)(2,1)S(1)}, bf16[128,2048]{1,0:T(8,128)(2,1)S(1)}, u32[]{:S(2)}, u32[]{:S(2)}) collective-permute-start(bf16[128,2048]{1,0:T(8,128)(2,1)S(1)} %add_share.18), channel_id=1, source_target_pairs={{0,8},{8,16},{16,24},{1,9},{9,17},{17,25},{2,10},{10,18},{18,26},{... | collective-permute-start | bytes 1572872 | tf_op jit(solution)/shard_map/ppermute | solution.py:255
  76.1 22.4 %collective-permute-start.21 = (bf16[128,2048]{1,0:T(8,128)(2,1)S(1)}, bf16[128,2048]{1,0:T(8,128)(2,1)S(1)}, u32[]{:S(2)}, u32[]{:S(2)}) collective-permute-start(bf16[128,2048]{1,0:T(8,128)(2,1)S(1)} %add_share.19), channel_id=1, source_target_pairs={{8,0},{16,8},{24,16},{9,1},{17,9},{25,17},{10,2},{18,10},{26,18},{... | collective-permute-start | bytes 1572872 | tf_op jit(solution)/shard_map/ppermute | solution.py:255
  82.8 26.3 %collective-permute-start.27 = (bf16[128,2048]{1,0:T(8,128)(2,1)S(1)}, bf16[128,2048]{1,0:T(8,128)(2,1)S(1)}, u32[]{:S(2)}, u32[]{:S(2)}) collective-permute-start(bf16[128,2048]{1,0:T(8,128)(2,1)S(1)} %add_share.20), channel_id=1, source_target_pairs={{0,8},{8,16},{16,24},{1,9},{9,17},{17,25},{2,10},{10,18},{18,26},{... | collective-permute-start | bytes 1572872 | tf_op jit(solution)/shard_map/ppermute | solution.py:255
  87.3 21.8 %collective-permute-start.28 = (bf16[128,2048]{1,0:T(8,128)(2,1)S(1)}, bf16[128,2048]{1,0:T(8,128)(2,1)S(1)}, u32[]{:S(2)}, u32[]{:S(2)}) collective-permute-start(bf16[128,2048]{1,0:T(8,128)(2,1)S(1)} %add_share.21), channel_id=1, source_target_pairs={{8,0},{16,8},{24,16},{9,1},{17,9},{25,17},{10,2},{18,10},{26,18},{... | collective-permute-start | bytes 1572872 | tf_op jit(solution)/shard_map/ppermute | solution.py:255
  94.0 25.5 %collective-permute-start.25 = (bf16[128,2048]{1,0:T(8,128)(2,1)S(1)}, bf16[128,2048]{1,0:T(8,128)(2,1)S(1)}, u32[]{:S(2)}, u32[]{:S(2)}) collective-permute-start(bf16[128,2048]{1,0:T(8,128)(2,1)S(1)} %add_share.22), channel_id=1, source_target_pairs={{0,8},{8,16},{16,24},{1,9},{9,17},{17,25},{2,10},{10,18},{18,26},{... | collective-permute-start | bytes 1572872 | tf_op jit(solution)/shard_map/ppermute | solution.py:255
  98.5 21.0 %collective-permute-start.26 = (bf16[128,2048]{1,0:T(8,128)(2,1)S(1)}, bf16[128,2048]{1,0:T(8,128)(2,1)S(1)}, u32[]{:S(2)}, u32[]{:S(2)}) collective-permute-start(bf16[128,2048]{1,0:T(8,128)(2,1)S(1)} %add_share.23), channel_id=1, source_target_pairs={{8,0},{16,8},{24,16},{9,1},{17,9},{25,17},{10,2},{18,10},{26,18},{... | collective-permute-start | bytes 1572872 | tf_op jit(solution)/shard_map/ppermute | solution.py:255
  (9 other events, 50.9 us)

commit v2 on v0

--- a/solution.py
+++ b/solution.py
@@ -4,8 +4,6 @@
 from jax.experimental import pallas as pl
 from jax.experimental.pallas import tpu as pltpu
 from jax.sharding import PartitionSpec as P
-
-PARTS = 2
 
 
 def after(value, first):
@@ -37,68 +35,65 @@
     )(*near, *far)
 
 
-def add_share(sources, cot, down_t, start, mine):
-    span = sum(count for _, _, count in sources)
-    like = sources[0][0]
-    width = like.shape[1]
+def goes_ahead(way):
+    return (lax.axis_index("col") & 1) == way
+
+
+def ring(value, way):
+    rows, cols = lax.axis_size("row"), lax.axis_size("col")
+    pairs = []
+    for row in range(rows):
+        for col in range(cols):
+            to = row + 1 if col & 1 == way else row - 1
+            if 0 <= to < rows:
+                pairs.append((row * cols + col, to * cols + col))
+    return lax.ppermute(value, ("row", "col"), pairs)
+
+
+def add_share(got, cot, down_t, way, step, first, tok_rows):
+    span, width = got.shape
     tile = 512 if width % 512 == 0 else width
 
-    def kernel(*refs):
-        got_refs, (cot_ref, down_ref, out_ref) = refs[: len(sources)], refs[len(sources) :]
-        is_sum = mine(lax.axis_index("row"))
-        places, at = [], 0
-        for ref, (_, first, count) in zip(got_refs, sources):
-            places.append((ref, slice(first, first + count), slice(at, at + count)))
-            at += count
+    def kernel(got_ref, cot_ref, down_ref, out_ref):
+        rows, row, ahead = lax.axis_size("row"), lax.axis_index("row"), goes_ahead(way)
+        is_sum = step > jnp.where(ahead, row + 1, rows - row)
+        start = jnp.where(ahead, rows + 1 - step, step - 1) * tok_rows + first
 
         @pl.when(is_sum)
         def _():
-            tokens = cot_ref[start : start + span, :]
+            tokens = cot_ref[pl.ds(pl.multiple_of(start, 16), span), :]
             for at in range(0, width, tile):
                 cut = slice(at, at + tile)
                 share = jnp.dot(tokens, down_ref[:, cut], preferred_element_type=jnp.float32)
-                for ref, source, here in places:
-                    total = ref[source, cut].astype(jnp.float32) + share[here]
-                    out_ref[here, cut] = total.astype(out_ref.dtype)
+                out_ref[:, cut] = (got_ref[:, cut].astype(jnp.float32) + share).astype(out_ref.dtype)
 
         @pl.when(jnp.logical_not(is_sum))
         def _():
-            for ref, source, here in places:
-                out_ref[here, :] = ref[source, :]
+            out_ref[...] = got_ref[...]
 
     whole = pl.BlockSpec(memory_space=pltpu.VMEM)
     return pl.pallas_call(
         kernel,
-        out_shape=jax.ShapeDtypeStruct((span, width), like.dtype),
-        in_specs=[whole] * (2 + len(sources)),
+        out_shape=jax.ShapeDtypeStruct(got.shape, got.dtype),
+        in_specs=[whole] * 3,
         out_specs=whole,
         compiler_params=pltpu.CompilerParams(vmem_limit_bytes=32 * 2**20),
         cost_estimate=pl.CostEstimate(
             flops=2 * span * down_t.size, bytes_accessed=4 * span * width, transcendentals=0
         ),
         name="add_share",
-    )(*(array for array, _, _ in sources), cot, down_t)
-
-
-def rows_of(pieces, start, count):
-    found, at = [], 0
-    for piece in pieces:
-        low, high = max(start, at), min(start + count, at + piece.shape[0])
-        if low < high:
-            found.append((piece, low - at, high - low))
-        at += piece.shape[0]
-    return found
-
-
-def weight_product(cot, own, fore, back, scale):
-    rows = len(fore) + 1
+    )(got, cot, down_t)
+
+
+def weight_product(cot, own, ways, scale):
+    rows = len(ways[0]) + 1
     tok_rows, width = own.shape
     tile = 512 if width % 512 == 0 else width
-    flat = [piece for pieces in fore + back for piece in pieces]
+    flat = [piece for steps in ways for pieces in steps for piece in pieces]
 
     def kernel(cot_ref, own_ref, *refs):
         ends, (out_ref, hidden_ref) = iter(refs[: len(flat)]), refs[len(flat) :]
-        fore_refs, back_refs = ([[next(ends) for _ in pieces] for pieces in way] for way in (fore, back))
+        way_refs = [[[next(ends) for _ in pieces] for pieces in steps] for steps in ways]
         row = lax.axis_index("row")
 
         def place(pieces, start, cut):
@@ -111,11 +106,14 @@
             cut = pl.ds(pl.multiple_of(at * tile, tile), tile)
             place([own_ref], 0, cut)
             for slot in range(1, rows):
-                for here, pieces in (
-                    (row + slot < rows, back_refs[slot - 1]),
-                    (row + slot >= rows, fore_refs[rows - slot - 1]),
-                ):
-                    pl.when(here)(lambda pieces=pieces, slot=slot: place(pieces, slot * tok_rows, cut))
+                for way, refs_of in enumerate(way_refs):
+                    ahead, from_next = goes_ahead(way), row + slot < rows
+                    for here, step in (
+                        (jnp.logical_and(from_next, jnp.logical_not(ahead)), slot),
+                        (jnp.logical_and(jnp.logical_not(from_next), ahead), rows - slot),
+                    ):
+                        pieces = refs_of[step - 1]
+                        pl.when(here)(lambda pieces=pieces, slot=slot: place(pieces, slot * tok_rows, cut))
             total = lax.dot_general(
                 cot_ref[...],
                 hidden_ref[...],
@@ -216,52 +214,45 @@
     tall = jnp.stack(tall[::-1])
     near = [tall, swap(tall, 2), swap(tall, 4), swap(tall, 6)]
     near[-1] = after(near[-1], first)
-    return lay_strips(near, [swap(block, 1) for block in near])
+    far = [swap(block, 1) for block in near]
+    return lay_strips(near, far)
 
 
 def per_device(gate_pre, up_pre, down_t, grad_out):
     rows = lax.axis_size("row")
-    row = lax.axis_index("row")
     tok_rows, width = gate_pre.shape
     norm_scale = (tok_rows * rows) ** (-0.5)
     wire = jnp.bfloat16 if rows <= 4 else jnp.float32
-    ahead = [(at, at + 1) for at in range(rows - 1)]
-    behind = [(at + 1, at) for at in range(rows - 1)]
-    span = tok_rows // PARTS
-
-    hidden, fore, back = [], [None, []], [None, []]
-    for start, count in ((0, span), (span, span)):
+    lead = tok_rows * 8 // 16
+    chains = ((0, lead), (lead, tok_rows - lead))
+
+    hidden, ways = [], ([[]], [[]])
+    for start, count in chains:
         gate_cut = gate_pre[start : start + count].astype(jnp.float32)
         up_cut = up_pre[start : start + count].astype(jnp.float32)
         hidden.append((gate_cut * jax.nn.sigmoid(gate_cut) * up_cut).astype(jnp.bfloat16))
-        fore[1].append(lax.ppermute(hidden[-1].astype(wire), "row", ahead))
-        back[1].append(lax.ppermute(hidden[-1].astype(wire), "row", behind))
-
-    cot = spread_cotangent(grad_out, hidden, (fore[1][:1], back[1][:1]))
+        for way, steps in enumerate(ways):
+            steps[0].append(ring(hidden[-1].astype(wire), way))
+
+    cot = spread_cotangent(grad_out, hidden, [steps[0][0] for steps in ways])
     turn = hidden[0]
     for step in range(2, rows + 1):
-        fore.append([None] * PARTS)
-        back.append([None] * PARTS)
-        for at in range(PARTS):
-            for ends, slot, mine, pairs in (
-                (fore, rows + 1 - step, lambda row, step=step: step > row + 1, ahead),
-                (back, step - 1, lambda row, step=step: step > rows - row, behind),
-            ):
-                sources = [
-                    (after(piece, turn), first, count)
-                    for piece, first, count in rows_of(ends[step - 1], at * span, span)
-                ]
-                turn = add_share(sources, cot, down_t, slot * tok_rows + at * span, mine)
-                ends[step][at] = lax.ppermute(turn, "row", pairs)
+        for steps in ways:
+            steps.append([])
+        for at, (first, _) in enumerate(chains):
+            for way, steps in enumerate(ways):
+                got = after(steps[-2][at], turn)
+                turn = add_share(got, cot, down_t, way, step, first, tok_rows)
+                steps[-1].append(ring(turn, way))
         late = turn
 
-    weight_grad = weight_product(cot, jnp.concatenate(hidden), fore[1:rows], back[1:rows], norm_scale)
+    weight_grad = weight_product(cot, jnp.concatenate(hidden), [steps[:-1] for steps in ways], norm_scale)
 
     own_share = jnp.dot(after(cot[:tok_rows], late), down_t, preferred_element_type=jnp.float32)
     own_share, gate_again, up_again = after((own_share, gate_pre, up_pre), turn)
     grads = None
-    for at in range(PARTS):
-        grads = finish(gate_again, up_again, own_share, fore[rows][at], back[rows][at], at * span, grads)
+    for at, (first, _) in enumerate(chains):
+        grads = finish(gate_again, up_again, own_share, ways[0][-1][at], ways[1][-1][at], first, grads)
     return *grads, weight_grad
 
 

time: 119 us -> 117 us (0.983)
  waiting for transfers between devices: 41.2 us -> 34.7 us
  starting transfers between devices: 56.1 us -> 60.3 us
    ppermute x16, waiting for transfers between devices: 29.3 us -> 23 us  [ring(): return lax.ppermute(value, ('row', 'col'), pairs)]
    ppermute x16, starting transfers between devices: 42.9 us -> 46.8 us  [ring(): return lax.ppermute(value, ('row', 'col'), pairs)]
where the time goes in v2:
time: 117 us; the launch traced here: 116 us
  starting transfers between devices  60.3 us (52%)
  waiting for transfers between devices  34.7 us (30%)
  Pallas kernels  15.4 us (13%)
  other arithmetic  2.33 us (2%)
  between operations  1.27 us (1%)
  matrix products  1.25 us (1%)
    ppermute x16, starting transfers between devices, ring(): return lax.ppermute(value, ('row', 'col'), pairs)  46.8 us
    ppermute x16, waiting for transfers between devices, ring(): return lax.ppermute(value, ('row', 'col'), pairs)  23 us
    ppermute x10, waiting for transfers between devices, swap(): lax.ppermute(value, 'col', [(at, at ^ bits) for at in range(lax.axis_size...  11.6 us
    ppermute x10, starting transfers between devices, swap(): lax.ppermute(value, 'col', [(at, at ^ bits) for at in range(lax.axis_size...  9.06 us
    pallas_call x1, Pallas kernels, weight_product(): pl.pallas_call(kernel, out_shape=jax.ShapeDtypeStruct((cot.shape[1], widt...  7.6 us
    pallas_call x12, Pallas kernels, add_share(): pl.pallas_call(kernel, out_shape=jax.ShapeDtypeStruct(got.shape, got.dtyp...  4.88 us
    ppermute x3, starting transfers between devices, across(): lax.ppermute(piece, 'row', [(at, at ^ bits) for at in range(rows)])  4.45 us
    pallas_call x2, Pallas kernels, finish(): pl.pallas_call(kernel, out_shape=[jax.ShapeDtypeStruct(gate_pre.shape, jn...  2.77 us
  transfers between devices with their start and end apart: 29, of which 14 were waited for; matrix products, arithmetic and copies ran while one was open for 3% of the time, Pallas kernels for 12%

profile of v2, /device:TPU:0, one launch (start us, length us, event | category | flops | bytes accessed | tf_op | source)
XLA Modules:
  0.0 116.4 jit_solution(14808720273466371075)
XLA Ops:
  1.6 3.0 %collective-permute-start = (bf16[64,512]{1,0:T(8,128)(2,1)S(1)}, bf16[64,512]{1,0:T(8,128)(2,1)S(1)}, u32[]{:S(2)}, u32[]{:S(2)}) collective-permute-start(bf16[64,512]{1,0:T(8,128)(2,1)S(1)} %get-tuple-element.60), channel_id=1, source_target_pairs={{0,2},{1,3},{2,0},{3,1},{4,6},{5,7},{6,4},{7,5},{8,10},{9,11},{10,... | collective-permute-start | bytes 196616 | tf_op jit(solution)/shard_map/ppermute | solution.py:181
  4.6 1.5 %collective-permute-start.1 = (bf16[64,512]{1,0:T(8,128)(2,1)S(1)}, bf16[64,512]{1,0:T(8,128)(2,1)S(1)}, u32[]{:S(2)}, u32[]{:S(2)}) collective-permute-start(bf16[64,512]{1,0:T(8,128)(2,1)S(1)} %get-tuple-element.62), channel_id=1, source_target_pairs={{0,4},{1,5},{2,6},{3,7},{4,0},{5,1},{6,2},{7,3},{8,12},{9,13},{10,... | collective-permute-start | bytes 196616 | tf_op jit(solution)/shard_map/ppermute | solution.py:181
  6.2 2.2 %fusion.8 = (bf16[128,2048]{1,0:T(8,128)(2,1)S(1)}, bf16[128,2048]{1,0:T(8,128)(2,1)S(1)}) fusion(bf16[256,2048]{1,0:T(8,128)(2,1)} %refs_1_.1, bf16[256,2048]{1,0:T(8,128)(2,1)} %refs_0_.1), kind=kLoop, calls=%fused_computation.13 | loop fusion | flops 4194304 | bytes 3145728 | tf_op jit(solution)/shard_map/convert_element_type | solution.py:233
  8.9 2.4 %collective-permute-done.2 = bf16[64,512]{1,0:T(8,128)(2,1)S(1)} collective-permute-done((bf16[64,512]{1,0:T(8,128)(2,1)S(1)}, bf16[64,512]{1,0:T(8,128)(2,1)S(1)}, u32[]{:S(2)}, u32[]{:S(2)}) %collective-permute-start.2) | collective-permute-done | bytes 65568 | tf_op jit(solution)/shard_map/ppermute | solution.py:181
  11.4 1.6 %collective-permute-start.3 = (bf16[64,512]{1,0:T(8,128)(2,1)S(1)}, bf16[64,512]{1,0:T(8,128)(2,1)S(1)}, u32[]{:S(2)}, u32[]{:S(2)}) collective-permute-start(bf16[64,512]{1,0:T(8,128)(2,1)S(1)} %get-tuple-element.58), channel_id=1, source_target_pairs={{0,8},{8,0},{16,24},{24,16},{1,9},{9,1},{17,25},{25,17},{2,10},{10... | collective-permute-start | bytes 196616 | tf_op jit(solution)/shard_map/ppermute | solution.py:211
  13.0 2.6 %collective-permute-start.4 = (bf16[64,512]{1,0:T(8,128)(2,1)S(1)}, bf16[64,512]{1,0:T(8,128)(2,1)S(1)}, u32[]{:S(2)}, u32[]{:S(2)}) collective-permute-start(bf16[64,512]{1,0:T(8,128)(2,1)S(1)} %get-tuple-element.57), channel_id=1, source_target_pairs={{0,16},{8,24},{16,0},{24,8},{1,17},{9,25},{17,1},{25,9},{2,18},{10... | collective-permute-start | bytes 196616 | tf_op jit(solution)/shard_map/ppermute | solution.py:211
  17.1 4.6 %collective-permute-start.9 = (bf16[128,2048]{1,0:T(8,128)(2,1)S(1)}, bf16[128,2048]{1,0:T(8,128)(2,1)S(1)}, u32[]{:S(2)}, u32[]{:S(2)}) collective-permute-start(bf16[128,2048]{1,0:T(8,128)(2,1)S(1)} %get-tuple-element.54), channel_id=1, source_target_pairs={{0,8},{2,10},{4,12},{6,14},{8,16},{9,1},{10,18},{11,3},{12,20},{13... | collective-permute-start | bytes 1572872 | tf_op jit(solution)/shard_map/ppermute | solution.py:50
  22.4 1.5 %collective-permute-start.6 = (bf16[4,64,512]{2,1,0:T(8,128)(2,1)S(1)}, bf16[4,64,512]{2,1,0:T(8,128)(2,1)S(1)}, u32[]{:S(2)}, u32[]{:S(2)}) collective-permute-start(bf16[4,64,512]{2,1,0:T(8,128)(2,1)S(1)} %pad_maximum_fusion.2.refs_0_), channel_id=1, source_target_pairs={{0,2},{1,3},{2,0},{3,1},{4,6},{5,7},{6,4},{7,5},{8,10},{9,11},{10,... | collective-permute-start | bytes 786440 | tf_op jit(solution)/shard_map/ppermute | solution.py:181
  23.9 1.5 %collective-permute-start.7 = (bf16[4,64,512]{2,1,0:T(8,128)(2,1)S(1)}, bf16[4,64,512]{2,1,0:T(8,128)(2,1)S(1)}, u32[]{:S(2)}, u32[]{:S(2)}) collective-permute-start(bf16[4,64,512]{2,1,0:T(8,128)(2,1)S(1)} %pad_maximum_fusion.2.refs_0_), channel_id=1, source_target_pairs={{0,4},{1,5},{2,6},{3,7},{4,0},{5,1},{6,2},{7,3},{8,12},{9,13},{10,... | collective-permute-start | bytes 786440 | tf_op jit(solution)/shard_map/ppermute | solution.py:181
  25.4 5.5 %collective-permute-done.8.refs_3_ = bf16[4,64,512]{2,1,0:T(8,128)(2,1)S(1)} collective-permute-done((bf16[4,64,512]{2,1,0:T(8,128)(2,1)S(1)}, bf16[4,64,512]{2,1,0:T(8,128)(2,1)S(1)}, u32[]{:S(2)}, u32[]{:S(2)}) %collective-permute-start.8) | collective-permute-done | bytes 262176 | tf_op jit(solution)/shard_map/ppermute | solution.py:181
  30.9 1.8 %collective-permute-done.6.refs_1_ = bf16[4,64,512]{2,1,0:T(8,128)(2,1)S(1)} collective-permute-done((bf16[4,64,512]{2,1,0:T(8,128)(2,1)S(1)}, bf16[4,64,512]{2,1,0:T(8,128)(2,1)S(1)}, u32[]{:S(2)}, u32[]{:S(2)}) %collective-permute-start.6) | collective-permute-done | bytes 262176 | tf_op jit(solution)/shard_map/ppermute | solution.py:181
  32.7 2.6 %collective-permute-start.16 = (bf16[128,2048]{1,0:T(8,128)(2,1)S(1)}, bf16[128,2048]{1,0:T(8,128)(2,1)S(1)}, u32[]{:S(2)}, u32[]{:S(2)}) collective-permute-start(bf16[128,2048]{1,0:T(8,128)(2,1)S(1)} %get-tuple-element.53), channel_id=1, source_target_pairs={{0,8},{2,10},{4,12},{6,14},{8,16},{9,1},{10,18},{11,3},{12,20},{13... | collective-permute-start | bytes 1572872 | tf_op jit(solution)/shard_map/ppermute | solution.py:50
  40.0 4.1 %collective-permute-start.20 = (bf16[128,2048]{1,0:T(8,128)(2,1)S(1)}, bf16[128,2048]{1,0:T(8,128)(2,1)S(1)}, u32[]{:S(2)}, u32[]{:S(2)}) collective-permute-start(bf16[128,2048]{1,0:T(8,128)(2,1)S(1)} %add_share.12), channel_id=1, source_target_pairs={{0,8},{2,10},{4,12},{6,14},{8,16},{9,1},{10,18},{11,3},{12,20},{13... | collective-permute-start | bytes 1572872 | tf_op jit(solution)/shard_map/ppermute | solution.py:50
  47.3 4.5 %collective-permute-start.18 = (bf16[128,2048]{1,0:T(8,128)(2,1)S(1)}, bf16[128,2048]{1,0:T(8,128)(2,1)S(1)}, u32[]{:S(2)}, u32[]{:S(2)}) collective-permute-start(bf16[128,2048]{1,0:T(8,128)(2,1)S(1)} %add_share.14), channel_id=1, source_target_pairs={{0,8},{2,10},{4,12},{6,14},{8,16},{9,1},{10,18},{11,3},{12,20},{13... | collective-permute-start | bytes 1572872 | tf_op jit(solution)/shard_map/ppermute | solution.py:50
  53.2 4.6 %collective-permute-done.20.got_ref.refs_2_ = bf16[128,2048]{1,0:T(8,128)(2,1)S(1)} collective-permute-done((bf16[128,2048]{1,0:T(8,128)(2,1)S(1)}, bf16[128,2048]{1,0:T(8,128)(2,1)S(1)}, u32[]{:S(2)}, u32[]{:S(2)}) %collective-permute-start.20) | collective-permute-done | bytes 524320 | tf_op jit(solution)/shard_map/ppermute | solution.py:50
  58.6 5.2 %collective-permute-start.24 = (bf16[128,2048]{1,0:T(8,128)(2,1)S(1)}, bf16[128,2048]{1,0:T(8,128)(2,1)S(1)}, u32[]{:S(2)}, u32[]{:S(2)}) collective-permute-start(bf16[128,2048]{1,0:T(8,128)(2,1)S(1)} %add_share.16), channel_id=1, source_target_pairs={{0,8},{2,10},{4,12},{6,14},{8,16},{9,1},{10,18},{11,3},{12,20},{13... | collective-permute-start | bytes 1572872 | tf_op jit(solution)/shard_map/ppermute | solution.py:50
  65.1 3.9 %collective-permute-done.18.got_ref.refs_3_ = bf16[128,2048]{1,0:T(8,128)(2,1)S(1)} collective-permute-done((bf16[128,2048]{1,0:T(8,128)(2,1)S(1)}, bf16[128,2048]{1,0:T(8,128)(2,1)S(1)}, u32[]{:S(2)}, u32[]{:S(2)}) %collective-permute-start.18) | collective-permute-done | bytes 524320 | tf_op jit(solution)/shard_map/ppermute | solution.py:50
  69.8 5.2 %collective-permute-start.22 = (bf16[128,2048]{1,0:T(8,128)(2,1)S(1)}, bf16[128,2048]{1,0:T(8,128)(2,1)S(1)}, u32[]{:S(2)}, u32[]{:S(2)}) collective-permute-start(bf16[128,2048]{1,0:T(8,128)(2,1)S(1)} %add_share.18), channel_id=1, source_target_pairs={{0,8},{2,10},{4,12},{6,14},{8,16},{9,1},{10,18},{11,3},{12,20},{13... | collective-permute-start | bytes 1572872 | tf_op jit(solution)/shard_map/ppermute | solution.py:50
  76.5 3.8 %collective-permute-done.24.got_ref.refs_4_ = bf16[128,2048]{1,0:T(8,128)(2,1)S(1)} collective-permute-done((bf16[128,2048]{1,0:T(8,128)(2,1)S(1)}, bf16[128,2048]{1,0:T(8,128)(2,1)S(1)}, u32[]{:S(2)}, u32[]{:S(2)}) %collective-permute-start.24) | collective-permute-done | bytes 524320 | tf_op jit(solution)/shard_map/ppermute | solution.py:50
  81.0 5.2 %collective-permute-start.27 = (bf16[128,2048]{1,0:T(8,128)(2,1)S(1)}, bf16[128,2048]{1,0:T(8,128)(2,1)S(1)}, u32[]{:S(2)}, u32[]{:S(2)}) collective-permute-start(bf16[128,2048]{1,0:T(8,128)(2,1)S(1)} %add_share.20), channel_id=1, source_target_pairs={{0,8},{2,10},{4,12},{6,14},{8,16},{9,1},{10,18},{11,3},{12,20},{13... | collective-permute-start | bytes 1572872 | tf_op jit(solution)/shard_map/ppermute | solution.py:50
  87.6 3.9 %collective-permute-done.22.got_ref.refs_5_ = bf16[128,2048]{1,0:T(8,128)(2,1)S(1)} collective-permute-done((bf16[128,2048]{1,0:T(8,128)(2,1)S(1)}, bf16[128,2048]{1,0:T(8,128)(2,1)S(1)}, u32[]{:S(2)}, u32[]{:S(2)}) %collective-permute-start.22) | collective-permute-done | bytes 524320 | tf_op jit(solution)/shard_map/ppermute | solution.py:50
  92.3 5.2 %collective-permute-start.25 = (bf16[128,2048]{1,0:T(8,128)(2,1)S(1)}, bf16[128,2048]{1,0:T(8,128)(2,1)S(1)}, u32[]{:S(2)}, u32[]{:S(2)}) collective-permute-start(bf16[128,2048]{1,0:T(8,128)(2,1)S(1)} %add_share.22), channel_id=1, source_target_pairs={{0,8},{2,10},{4,12},{6,14},{8,16},{9,1},{10,18},{11,3},{12,20},{13... | collective-permute-start | bytes 1572872 | tf_op jit(solution)/shard_map/ppermute | solution.py:50
  100.3 7.6 %weight_product.1 = bf16[1024,2048]{1,0:T(8,128)(2,1)} custom-call(bf16[1024,1024]{1,0:T(8,128)(2,1)S(1)} %lay_strips.1.cot_ref, bf16[256,2048]{1,0:T(8,128)(2,1)S(1)} %pad_maximum_fusion.own_ref, bf16[128,2048]{1,0:T(8,128)(2,1)S(1)} %collective-permute-done.9.got_ref.refs_0_, bf16[128,2048]{1,0:T(8,128)(2,1)S(1)} %collective-permute-done.16.got_ref.refs_1_, ...), custom_call_target="tpu_custom_call" | custom-call | flops 4294967296 | bytes 8388608 | tf_op jit(solution)/shard_map/weight_product/pallas_call | solution.py:126
  109.3 5.5 %collective-permute-done.26.refs_4_ = bf16[128,2048]{1,0:T(8,128)(2,1)S(1)} collective-permute-done((bf16[128,2048]{1,0:T(8,128)(2,1)S(1)}, bf16[128,2048]{1,0:T(8,128)(2,1)S(1)}, u32[]{:S(2)}, u32[]{:S(2)}) %collective-permute-start.26) | collective-permute-done | bytes 524320 | tf_op jit(solution)/shard_map/ppermute | solution.py:50
  (64 shorter events, 25.5 us)
Async XLA Ops:
  1.6 6.8 %collective-permute-start = (bf16[64,512]{1,0:T(8,128)(2,1)S(1)}, bf16[64,512]{1,0:T(8,128)(2,1)S(1)}, u32[]{:S(2)}, u32[]{:S(2)}) collective-permute-start(bf16[64,512]{1,0:T(8,128)(2,1)S(1)} %get-tuple-element.60), channel_id=1, source_target_pairs={{0,2},{1,3},{2,0},{3,1},{4,6},{5,7},{6,4},{7,5},{8,10},{9,11},{10,... | collective-permute-start | bytes 196616 | tf_op jit(solution)/shard_map/ppermute | solution.py:181
  11.4 10.3 %collective-permute-start.3 = (bf16[64,512]{1,0:T(8,128)(2,1)S(1)}, bf16[64,512]{1,0:T(8,128)(2,1)S(1)}, u32[]{:S(2)}, u32[]{:S(2)}) collective-permute-start(bf16[64,512]{1,0:T(8,128)(2,1)S(1)} %get-tuple-element.58), channel_id=1, source_target_pairs={{0,8},{8,0},{16,24},{24,16},{1,9},{9,1},{17,25},{25,17},{2,10},{10... | collective-permute-start | bytes 196616 | tf_op jit(solution)/shard_map/ppermute | solution.py:211
  13.0 8.7 %collective-permute-start.4 = (bf16[64,512]{1,0:T(8,128)(2,1)S(1)}, bf16[64,512]{1,0:T(8,128)(2,1)S(1)}, u32[]{:S(2)}, u32[]{:S(2)}) collective-permute-start(bf16[64,512]{1,0:T(8,128)(2,1)S(1)} %get-tuple-element.57), channel_id=1, source_target_pairs={{0,16},{8,24},{16,0},{24,8},{1,17},{9,25},{17,1},{25,9},{2,18},{10... | collective-permute-start | bytes 196616 | tf_op jit(solution)/shard_map/ppermute | solution.py:211
  15.6 6.2 %collective-permute-start.5 = (bf16[64,512]{1,0:T(8,128)(2,1)S(1)}, bf16[64,512]{1,0:T(8,128)(2,1)S(1)}, u32[]{:S(2)}, u32[]{:S(2)}) collective-permute-start(bf16[64,512]{1,0:T(8,128)(2,1)S(1)} %get-tuple-element.56), channel_id=1, source_target_pairs={{0,24},{8,16},{16,8},{24,0},{1,25},{9,17},{17,9},{25,1},{2,26},{10... | collective-permute-start | bytes 196616 | tf_op jit(solution)/shard_map/ppermute | solution.py:211
  15.9 20.8 %collective-permute-start.10 = (bf16[128,2048]{1,0:T(8,128)(2,1)S(1)}, bf16[128,2048]{1,0:T(8,128)(2,1)S(1)}, u32[]{:S(2)}, u32[]{:S(2)}) collective-permute-start(bf16[128,2048]{1,0:T(8,128)(2,1)S(1)} %get-tuple-element.54), channel_id=1, source_target_pairs={{1,9},{3,11},{5,13},{7,15},{8,0},{9,17},{10,2},{11,19},{12,4},{13,... | collective-permute-start | bytes 1572872 | tf_op jit(solution)/shard_map/ppermute | solution.py:50
  17.1 20.0 %collective-permute-start.9 = (bf16[128,2048]{1,0:T(8,128)(2,1)S(1)}, bf16[128,2048]{1,0:T(8,128)(2,1)S(1)}, u32[]{:S(2)}, u32[]{:S(2)}) collective-permute-start(bf16[128,2048]{1,0:T(8,128)(2,1)S(1)} %get-tuple-element.54), channel_id=1, source_target_pairs={{0,8},{2,10},{4,12},{6,14},{8,16},{9,1},{10,18},{11,3},{12,20},{13... | collective-permute-start | bytes 1572872 | tf_op jit(solution)/shard_map/ppermute | solution.py:50
  21.8 9.1 %collective-permute-start.8 = (bf16[4,64,512]{2,1,0:T(8,128)(2,1)S(1)}, bf16[4,64,512]{2,1,0:T(8,128)(2,1)S(1)}, u32[]{:S(2)}, u32[]{:S(2)}) collective-permute-start(bf16[4,64,512]{2,1,0:T(8,128)(2,1)S(1)} %pad_maximum_fusion.2.refs_0_), channel_id=1, source_target_pairs={{0,6},{1,7},{2,4},{3,5},{4,2},{5,3},{6,0},{7,1},{8,14},{9,15},{10,... | collective-permute-start | bytes 786440 | tf_op jit(solution)/shard_map/ppermute | solution.py:181
  22.4 10.3 %collective-permute-start.6 = (bf16[4,64,512]{2,1,0:T(8,128)(2,1)S(1)}, bf16[4,64,512]{2,1,0:T(8,128)(2,1)S(1)}, u32[]{:S(2)}, u32[]{:S(2)}) collective-permute-start(bf16[4,64,512]{2,1,0:T(8,128)(2,1)S(1)} %pad_maximum_fusion.2.refs_0_), channel_id=1, source_target_pairs={{0,2},{1,3},{2,0},{3,1},{4,6},{5,7},{6,4},{7,5},{8,10},{9,11},{10,... | collective-permute-start | bytes 786440 | tf_op jit(solution)/shard_map/ppermute | solution.py:181
  23.9 11.5 %collective-permute-start.7 = (bf16[4,64,512]{2,1,0:T(8,128)(2,1)S(1)}, bf16[4,64,512]{2,1,0:T(8,128)(2,1)S(1)}, u32[]{:S(2)}, u32[]{:S(2)}) collective-permute-start(bf16[4,64,512]{2,1,0:T(8,128)(2,1)S(1)} %pad_maximum_fusion.2.refs_0_), channel_id=1, source_target_pairs={{0,4},{1,5},{2,6},{3,7},{4,0},{5,1},{6,2},{7,3},{8,12},{9,13},{10,... | collective-permute-start | bytes 786440 | tf_op jit(solution)/shard_map/ppermute | solution.py:181
  30.9 6.3 %collective-permute-start.11 = (bf16[4,64,512]{2,1,0:T(8,128)(2,1)S(1)}, bf16[4,64,512]{2,1,0:T(8,128)(2,1)S(1)}, u32[]{:S(2)}, u32[]{:S(2)}) collective-permute-start(bf16[4,64,512]{2,1,0:T(8,128)(2,1)S(1)} %pad_maximum_fusion.2.refs_0_), channel_id=1, source_target_pairs={{0,1},{1,0},{2,3},{3,2},{4,5},{5,4},{6,7},{7,6},{8,9},{9,8},{10,11... | collective-permute-start | bytes 786440 | tf_op jit(solution)/shard_map/ppermute | solution.py:181
  32.7 13.9 %collective-permute-start.16 = (bf16[128,2048]{1,0:T(8,128)(2,1)S(1)}, bf16[128,2048]{1,0:T(8,128)(2,1)S(1)}, u32[]{:S(2)}, u32[]{:S(2)}) collective-permute-start(bf16[128,2048]{1,0:T(8,128)(2,1)S(1)} %get-tuple-element.53), channel_id=1, source_target_pairs={{0,8},{2,10},{4,12},{6,14},{8,16},{9,1},{10,18},{11,3},{12,20},{13... | collective-permute-start | bytes 1572872 | tf_op jit(solution)/shard_map/ppermute | solution.py:50
  35.3 16.5 %collective-permute-start.15 = (bf16[128,2048]{1,0:T(8,128)(2,1)S(1)}, bf16[128,2048]{1,0:T(8,128)(2,1)S(1)}, u32[]{:S(2)}, u32[]{:S(2)}) collective-permute-start(bf16[128,2048]{1,0:T(8,128)(2,1)S(1)} %get-tuple-element.53), channel_id=1, source_target_pairs={{1,9},{3,11},{5,13},{7,15},{8,0},{9,17},{10,2},{11,19},{12,4},{13,... | collective-permute-start | bytes 1572872 | tf_op jit(solution)/shard_map/ppermute | solution.py:50
  40.0 17.9 %collective-permute-start.20 = (bf16[128,2048]{1,0:T(8,128)(2,1)S(1)}, bf16[128,2048]{1,0:T(8,128)(2,1)S(1)}, u32[]{:S(2)}, u32[]{:S(2)}) collective-permute-start(bf16[128,2048]{1,0:T(8,128)(2,1)S(1)} %add_share.12), channel_id=1, source_target_pairs={{0,8},{2,10},{4,12},{6,14},{8,16},{9,1},{10,18},{11,3},{12,20},{13... | collective-permute-start | bytes 1572872 | tf_op jit(solution)/shard_map/ppermute | solution.py:50
  44.1 19.7 %collective-permute-start.19 = (bf16[128,2048]{1,0:T(8,128)(2,1)S(1)}, bf16[128,2048]{1,0:T(8,128)(2,1)S(1)}, u32[]{:S(2)}, u32[]{:S(2)}) collective-permute-start(bf16[128,2048]{1,0:T(8,128)(2,1)S(1)} %add_share.13), channel_id=1, source_target_pairs={{1,9},{3,11},{5,13},{7,15},{8,0},{9,17},{10,2},{11,19},{12,4},{13,... | collective-permute-start | bytes 1572872 | tf_op jit(solution)/shard_map/ppermute | solution.py:50
  47.3 21.7 %collective-permute-start.18 = (bf16[128,2048]{1,0:T(8,128)(2,1)S(1)}, bf16[128,2048]{1,0:T(8,128)(2,1)S(1)}, u32[]{:S(2)}, u32[]{:S(2)}) collective-permute-start(bf16[128,2048]{1,0:T(8,128)(2,1)S(1)} %add_share.14), channel_id=1, source_target_pairs={{0,8},{2,10},{4,12},{6,14},{8,16},{9,1},{10,18},{11,3},{12,20},{13... | collective-permute-start | bytes 1572872 | tf_op jit(solution)/shard_map/ppermute | solution.py:50
  51.9 23.1 %collective-permute-start.17 = (bf16[128,2048]{1,0:T(8,128)(2,1)S(1)}, bf16[128,2048]{1,0:T(8,128)(2,1)S(1)}, u32[]{:S(2)}, u32[]{:S(2)}) collective-permute-start(bf16[128,2048]{1,0:T(8,128)(2,1)S(1)} %add_share.15), channel_id=1, source_target_pairs={{1,9},{3,11},{5,13},{7,15},{8,0},{9,17},{10,2},{11,19},{12,4},{13,... | collective-permute-start | bytes 1572872 | tf_op jit(solution)/shard_map/ppermute | solution.py:50
  58.6 21.7 %collective-permute-start.24 = (bf16[128,2048]{1,0:T(8,128)(2,1)S(1)}, bf16[128,2048]{1,0:T(8,128)(2,1)S(1)}, u32[]{:S(2)}, u32[]{:S(2)}) collective-permute-start(bf16[128,2048]{1,0:T(8,128)(2,1)S(1)} %add_share.16), channel_id=1, source_target_pairs={{0,8},{2,10},{4,12},{6,14},{8,16},{9,1},{10,18},{11,3},{12,20},{13... | collective-permute-start | bytes 1572872 | tf_op jit(solution)/shard_map/ppermute | solution.py:50
  63.8 22.4 %collective-permute-start.23 = (bf16[128,2048]{1,0:T(8,128)(2,1)S(1)}, bf16[128,2048]{1,0:T(8,128)(2,1)S(1)}, u32[]{:S(2)}, u32[]{:S(2)}) collective-permute-start(bf16[128,2048]{1,0:T(8,128)(2,1)S(1)} %add_share.17), channel_id=1, source_target_pairs={{1,9},{3,11},{5,13},{7,15},{8,0},{9,17},{10,2},{11,19},{12,4},{13,... | collective-permute-start | bytes 1572872 | tf_op jit(solution)/shard_map/ppermute | solution.py:50
  69.8 21.7 %collective-permute-start.22 = (bf16[128,2048]{1,0:T(8,128)(2,1)S(1)}, bf16[128,2048]{1,0:T(8,128)(2,1)S(1)}, u32[]{:S(2)}, u32[]{:S(2)}) collective-permute-start(bf16[128,2048]{1,0:T(8,128)(2,1)S(1)} %add_share.18), channel_id=1, source_target_pairs={{0,8},{2,10},{4,12},{6,14},{8,16},{9,1},{10,18},{11,3},{12,20},{13... | collective-permute-start | bytes 1572872 | tf_op jit(solution)/shard_map/ppermute | solution.py:50
  75.1 22.4 %collective-permute-start.21 = (bf16[128,2048]{1,0:T(8,128)(2,1)S(1)}, bf16[128,2048]{1,0:T(8,128)(2,1)S(1)}, u32[]{:S(2)}, u32[]{:S(2)}) collective-permute-start(bf16[128,2048]{1,0:T(8,128)(2,1)S(1)} %add_share.19), channel_id=1, source_target_pairs={{1,9},{3,11},{5,13},{7,15},{8,0},{9,17},{10,2},{11,19},{12,4},{13,... | collective-permute-start | bytes 1572872 | tf_op jit(solution)/shard_map/ppermute | solution.py:50
  81.0 26.9 %collective-permute-start.27 = (bf16[128,2048]{1,0:T(8,128)(2,1)S(1)}, bf16[128,2048]{1,0:T(8,128)(2,1)S(1)}, u32[]{:S(2)}, u32[]{:S(2)}) collective-permute-start(bf16[128,2048]{1,0:T(8,128)(2,1)S(1)} %add_share.20), channel_id=1, source_target_pairs={{0,8},{2,10},{4,12},{6,14},{8,16},{9,1},{10,18},{11,3},{12,20},{13... | collective-permute-start | bytes 1572872 | tf_op jit(solution)/shard_map/ppermute | solution.py:50
  86.3 21.6 %collective-permute-start.28 = (bf16[128,2048]{1,0:T(8,128)(2,1)S(1)}, bf16[128,2048]{1,0:T(8,128)(2,1)S(1)}, u32[]{:S(2)}, u32[]{:S(2)}) collective-permute-start(bf16[128,2048]{1,0:T(8,128)(2,1)S(1)} %add_share.21), channel_id=1, source_target_pairs={{1,9},{3,11},{5,13},{7,15},{8,0},{9,17},{10,2},{11,19},{12,4},{13,... | collective-permute-start | bytes 1572872 | tf_op jit(solution)/shard_map/ppermute | solution.py:50
  92.3 22.6 %collective-permute-start.25 = (bf16[128,2048]{1,0:T(8,128)(2,1)S(1)}, bf16[128,2048]{1,0:T(8,128)(2,1)S(1)}, u32[]{:S(2)}, u32[]{:S(2)}) collective-permute-start(bf16[128,2048]{1,0:T(8,128)(2,1)S(1)} %add_share.22), channel_id=1, source_target_pairs={{0,8},{2,10},{4,12},{6,14},{8,16},{9,1},{10,18},{11,3},{12,20},{13... | collective-permute-start | bytes 1572872 | tf_op jit(solution)/shard_map/ppermute | solution.py:50
  97.7 17.1 %collective-permute-start.26 = (bf16[128,2048]{1,0:T(8,128)(2,1)S(1)}, bf16[128,2048]{1,0:T(8,128)(2,1)S(1)}, u32[]{:S(2)}, u32[]{:S(2)}) collective-permute-start(bf16[128,2048]{1,0:T(8,128)(2,1)S(1)} %add_share.23), channel_id=1, source_target_pairs={{1,9},{3,11},{5,13},{7,15},{8,0},{9,17},{10,2},{11,19},{12,4},{13,... | collective-permute-start | bytes 1572872 | tf_op jit(solution)/shard_map/ppermute | solution.py:50
  (8 other events, 36.1 us)
